TPU v7x, 256 devices: a whole 4x4x8 slice. The times are simulated.
256 devices in a mesh: dp: 4 (over y_hi, core), vocab: 64 (over x, z, y_lo).
Axes of the slice: x: 4, y: 4 (y_hi: 2, y_lo: 2; y = y_hi * 2 + y_lo), z: 8, core: 2. Of those that a mesh axis runs over, the one named last changes fastest.
Arguments:
- hidden: bfloat16 [512, 8192], P('dp'), may hold values from -6 to 6
- head: bfloat16 [8192, 81920], P('dp', 'vocab'), may hold values from -4 to 4
- token_ids: int32 [512], replicated, may hold values from 0 to 81919
- old_logp: float32 [512], replicated, may hold values from -600 to 1
- advantages: float32 [512], replicated, may hold values from -5 to 5
- lengths: int32 [8], replicated, may hold values from 1 to 64, 256 in all
Outputs:
- log_ratio: float32 [512], P('dp')
- entropy: float32 [512], P('dp')
- grad_hidden: bfloat16 [512, 8192], P('vocab', 'dp')
- grad_head: bfloat16 [8192, 81920], P('dp', 'vocab')
Inputs may be any that keep to these rules, and one draw needn't show every extreme that they name: The 8 lengths sum to exactly 256, and the largest is exactly 64.
All inputs are finite; a program needn't handle non-finite values.
Results may differ from a plain program's by a relative error of at most 0.013.
Values may be sent and summed in bfloat16 or wider, within the bound.
A program may use at most 64 MiB of HBM per device.

v0:
```python
import jax
import jax.numpy as jnp
from jax import lax
from jax.sharding import PartitionSpec as P

kl_weight = 0.2
entropy_weight = 0.1


def lookup(table, index):
    count = table.shape[0]
    hits = index[:, None] == jnp.arange(count, dtype=jnp.int32)[None, :]
    return jnp.sum(jnp.where(hits, table[None, :], 0), axis=1)


def local(hidden, head, token_ids, old_logp, advantages, lengths):
    groups = lax.axis_size("dp")
    group = lax.axis_index("dp")
    shard = lax.axis_index("vocab")
    group_rows = hidden.shape[0]
    vocab_dev = head.shape[1]
    tokens = group_rows * groups
    seq_count = lengths.shape[0]
    resp = tokens // seq_count
    positions = jnp.arange(tokens, dtype=jnp.int32)
    sequence = positions // resp
    offset = positions % resp
    seq_len = lookup(lengths, sequence)
    live = offset < seq_len
    spread = lax.all_to_all(hidden, "dp", split_axis=1, concat_axis=0, tiled=True)
    my_rows = group * group_rows + jnp.arange(group_rows, dtype=jnp.int32)
    logits = lax.psum_scatter(
        jnp.dot(spread, head, preferred_element_type=jnp.float32),
        "dp",
        scatter_dimension=0,
        tiled=True,
    )
    row_ids = jnp.take(token_ids, my_rows)
    row_old = jnp.take(old_logp, my_rows)
    row_adv = jnp.take(advantages, my_rows)
    row_live = jnp.take(live, my_rows).astype(jnp.float32)
    columns = jnp.arange(vocab_dev, dtype=jnp.int32)
    target_hit = columns[None, :] == (row_ids - shard * vocab_dev)[:, None]
    target_part = jnp.sum(jnp.where(target_hit, logits, 0.0), axis=1)
    local_top = jnp.max(logits, axis=1)
    top = lax.pmax(local_top, "vocab")
    scaled = jnp.exp(logits - top[:, None])
    total, weighted, target = lax.psum(
        (jnp.sum(scaled, axis=1), jnp.sum(scaled * logits, axis=1), target_part), "vocab"
    )
    lse = top + jnp.log(total)
    entropy_all = lse - weighted / total
    log_ratio_all = target - lse - row_old
    ratio = jnp.exp(log_ratio_all)
    slope = (kl_weight - row_adv) * ratio - kl_weight
    probs = jnp.exp(logits - lse[:, None])
    onehot = target_hit.astype(jnp.float32)
    dlogits = row_live[:, None] * (
        slope[:, None] * (onehot - probs)
        + entropy_weight * probs * (logits - lse[:, None] + entropy_all[:, None])
    )
    dlogits = dlogits.astype(jnp.bfloat16)
    ratio_out = row_live * log_ratio_all
    entropy_out = row_live * entropy_all
    piece = lax.all_gather(dlogits, "dp", axis=0, tiled=True)
    head_acc = lax.dot_general(
        spread, piece, (((0,), (0,)), ((), ())), preferred_element_type=jnp.float32
    )
    part = lax.dot_general(
        piece, head, (((1,), (1,)), ((), ())), preferred_element_type=jnp.float32
    )
    grad_head = head_acc.astype(jnp.bfloat16)
    grad_hidden = lax.psum_scatter(part, "vocab", scatter_dimension=0, tiled=True).astype(
        jnp.bfloat16
    )
    return (ratio_out, entropy_out, grad_hidden, grad_head)


def solution(mesh):
    in_specs = (P("dp", None), P("dp", "vocab"), P(), P(), P(), P())
    out_specs = (P("dp"), P("dp"), P("vocab", "dp"), P("dp", "vocab"))
    return jax.shard_map(local, mesh=mesh, in_specs=in_specs, out_specs=out_specs, check_vma=False)
```

profile of v0, /device:TPU:8, one launch (start us, length us, event | category | flops | bytes accessed | tf_op | source)
XLA Modules:
  0.0 766.8 jit_solution(1924167563102396445)
XLA Ops:
  7.2 0.0 copy-start
  7.2 0.0 reduce-scatter.3.cloned.1.call-start
  7.2 4.1 copy.15
  11.3 30.8 %all_to_all.19 = bf16[128,4,2048]{0,2,1:T(8,128)(2,1)S(1)} all-to-all(bf16[128,4,2048]{0,2,1:T(8,128)(2,1)} %bitcast.14), channel_id=1, replica_groups=mesh['dp'=4,'vocab'=64] {'dp'}, dimensions={1} | all-to-all | bytes 4194304 | tf_op jit(solution)/shard_map/all_to_all | solution.py:30
  42.1 2.7 copy.16
  44.8 7.5 fusion.12
  52.2 0.0 copy-start.1
  52.2 0.0 copy-start.4
  52.3 0.0 copy-start.2
  52.3 0.0 reduce-scatter.3.cloned.1.call-update
  52.3 0.0 all-gather.2.cloned.1.call-start
  52.4 0.0 copy-done
  52.4 1.3 gather_fusion.3
  53.6 0.0 copy-done.1
  53.7 1.3 gather_fusion.2
  55.0 0.0 copy-done.4
  55.0 0.1 select_reduce_fusion.1
  55.1 1.2 gather_fusion
  56.3 0.0 copy-done.2
  56.3 1.3 gather_fusion.1
  57.6 41.9 %reduce-scatter.3.cloned.1.call-done = f32[128,1280]{1,0:T(8,128)} async-done(((f32[512,1280]{1,0:T(8,128)}), f32[128,1280]{1,0:T(8,128)}) %reduce-scatter.3.cloned.1.call-update) | async-done | bytes 655376 | tf_op jit(solution)/shard_map/reduce_scatter | solution.py:32
  99.5 1.2 reduce_max.9
  100.7 154.4 %pmax.7 = f32[128]{0:T(128)S(1)} all-reduce(f32[128]{0:T(128)S(1)} %reduce_max.9), channel_id=1, replica_groups=mesh['dp'=4,'vocab'=64] {'vocab'}, use_global_device_ids=true, to_apply=%region_5.6 | all-reduce | flops 128 | bytes 1024 | tf_op jit(solution)/shard_map/pmax | solution.py:46
  255.2 1.4 multiply_reduce_fusion
  256.6 157.1 %all-reduce = (f32[128]{0:T(128)S(1)}, f32[128]{0:T(128)S(1)}, f32[128]{0:T(128)S(1)}) all-reduce(f32[128]{0:T(128)S(1)} %get-tuple-element.23, f32[128]{0:T(128)S(1)} %get-tuple-element.22, f32[128]{0:T(128)S(1)} %get-tuple-element.21), channel_id=1, replica_groups=mesh['dp'=4,'vocab'=64] {'vocab'}, use_global_device_ids=true, to_apply=%region_3.4 | all-reduce | flops 384 | bytes 3072 | tf_op jit(solution)/shard_map/psum | solution.py:48
  413.7 0.5 broadcast_select_fusion.1
  414.3 2.3 multiply_convert_fusion
  416.6 0.0 all-gather.2.cloned.1.call-update
  416.6 0.0 reduce-scatter.5.cloned.1.call-start
  416.7 16.8 %all-gather.2.cloned.1.call-done = bf16[512,1280]{1,0:T(8,128)(2,1)} async-done(((bf16[128,1280]{1,0:T(8,128)(2,1)}), bf16[512,1280]{1,0:T(8,128)(2,1)}) %all-gather.2.cloned.1.call-update) | async-done | bytes 1310736 | tf_op jit(solution)/shard_map/all_gather | solution.py:65
  433.4 7.8 %fusion.13 = f32[512,2048]{1,0:T(8,128)} fusion(bf16[512,1280]{1,0:T(8,128)(2,1)} %all-gather.2.cloned.1.call-done, bf16[2048,1280]{1,0:T(8,128)(2,1)} %param.9), kind=kOutput, calls=%fused_computation.43 | convolution fusion | flops 2684354560 | bytes 10747904 | tf_op jit(solution)/shard_map/dot_general | solution.py:69
  441.2 0.0 copy-start.3
  441.2 0.0 copy-start.5
  441.2 0.0 reduce-scatter.5.cloned.1.call-update
  441.3 1.6 copy-done.3
  442.8 0.4 copy-done.5
  443.2 4.7 fusion
  447.9 7.9 %copy.17 = bf16[2048,1280]{1,0:T(8,128)(2,1)} copy(bf16[2048,1280]{0,1:T(8,128)(2,1)} %fusion) | data formatting | bytes 10485760
  455.7 303.1 %reduce-scatter.5.cloned.1.call-done = f32[8,2048]{1,0:T(8,128)} async-done(((f32[512,2048]{1,0:T(8,128)}), f32[8,2048]{1,0:T(8,128)}) %reduce-scatter.5.cloned.1.call-update) | async-done | bytes 65552 | tf_op jit(solution)/shard_map/reduce_scatter | solution.py:73
  758.8 1.5 convert_element_type.25
  (9 shorter events, 0.1 us)
Async XLA Ops:
  7.2 45.2 %copy-start = (f32[512]{0:T(512)S(1)}, f32[512]{0:T(512)}, u32[]{:S(2)}) copy-start(f32[512]{0:T(512)} %param.12) | copy-start | bytes 6148
  7.2 92.4 %reduce-scatter.3.cloned.1.call-start = ((), (), s32[]{:S(2)}) async-start(), calls=%async_computation.3 | async-start | bytes 3276800 | tf_op jit(solution)/shard_map/reduce_scatter | solution.py:32
  52.2 1.4 copy-start.1
  52.2 2.7 copy-start.4
  52.3 4.1 copy-start.2
  52.3 381.1 %all-gather.2.cloned.1.call-start = ((), (), s32[]{:S(2)}) async-start(), calls=%async_computation.4 | async-start | bytes 1638400 | tf_op jit(solution)/shard_map/all_gather | solution.py:65
  416.6 342.2 %reduce-scatter.5.cloned.1.call-start = ((), (), s32[]{:S(2)}) async-start(), calls=%async_computation.5 | async-start | bytes 4259840 | tf_op jit(solution)/shard_map/reduce_scatter | solution.py:73
  441.2 1.6 copy-start.3
  441.2 1.9 copy-start.5
Sparse Core Ops, SparseCore 0:
  52.4 47.0 reduce-scatter.2
  416.7 16.6 all-gather.1
  441.4 317.3 reduce-scatter.4
where the time goes:
time: 772 us; the launch traced here: 767 us
  waiting for transfers between devices  362 us (47%)
  blocking collectives  342 us (44%)
  local copies, waits for them, and re-layouts  21.6 us (3%)
  matrix products  20 us (3%)
  between operations  13.9 us (2%)
    reduce_scatter x1, waiting for transfers between devices, local(): lax.psum_scatter(part, 'vocab', scatter_dimension=0, tiled=True)  303 us
    psum x1, blocking collectives, local(): lax.psum((jnp.sum(scaled, axis=1), jnp.sum(scaled * logits, axis=1), targ...  157 us
    pmax x1, blocking collectives, local(): top = lax.pmax(local_top, 'vocab')  154 us
    reduce_scatter x1, waiting for transfers between devices, local(): lax.psum_scatter(jnp.dot(spread, head, preferred_element_type=jnp.float32...  41.9 us
    all_to_all x1, blocking collectives, local(): lax.all_to_all(hidden, 'dp', split_axis=1, concat_axis=0, tiled=True)  30.8 us
    all_gather x1, waiting for transfers between devices, local(): piece = lax.all_gather(dlogits, 'dp', axis=0, tiled=True)  16.8 us
  transfers between devices with their start and end apart: 3, of which 3 were waited for; matrix products, arithmetic and copies ran while one was open for 2% of the time, Pallas kernels for 0%

commit v1 on v0

v1 whole, which is shorter than its diff:
```python
import functools

import jax
import jax.numpy as jnp
from jax import lax
from jax.experimental import pallas as pl
from jax.experimental.pallas import tpu as pltpu
from jax.sharding import PartitionSpec as P

kl_weight = 0.2
entropy_weight = 0.1

F32 = jnp.float32
BF16 = jnp.bfloat16
MESH = pl.DeviceIdType.MESH

RESP = 64
SLOTS = 512
ROWS = 256
GROUP = 128
DEPTH = 2048
COLS = 1280
CC = 256
NC = COLS // CC
TF = 512
NT = DEPTH // TF
TILES_XY = (0, 1, 2)


def slot_of(lens, row):
    end = 0
    slot = row
    for s in range(len(lens) - 1):
        end = end + lens[s]
        slot = slot + jnp.where(row >= end, RESP - lens[s], 0)
    return slot


def iota(shape, dim):
    return lax.broadcasted_iota(jnp.int32, shape, dim)


def merge(parts):
    top = functools.reduce(jnp.maximum, [p[0:1] for p in parts])
    scales = [jnp.exp(p[0:1] - top) for p in parts]
    total = sum(p[1:2] * s for p, s in zip(parts, scales))
    weighted = sum(p[2:3] * s for p, s in zip(parts, scales))
    target = sum(p[3:4] for p in parts)
    return top, total, weighted, target


def main_kernel(
    len_ref, tok_ref, old_ref, adv_ref, hid_ref, head_ref,
    comp_out, dl_out, lr_out, en_out, gh_out,
    spread, head_v, comp, lp, rxc, sy, ryy, logit, st1, st2, stz, stxy, dl_all, sm_all, dle, part, rx1, s2, rx2, gh_acc,
    loc_sem, hs_s, hs_r, lc_s, lc_r, ly_s, ly_r, z_s, z_r, xy_s, xy_r, d_s, d_r, m_s, m_r, a_s, a_r, b_s, b_r, out_sem,
):
    dp = lax.axis_index("dp")
    v = lax.axis_index("vocab")
    y_hi, core = dp // 2, dp % 2
    x, z, y_lo = v // 16, (v // 2) % 8, v % 2
    m = x * 2 + y_lo

    def dp_id(d):
        return {"dp": d, "vocab": v}

    def z_id(k):
        return {"dp": dp, "vocab": x * 16 + ((z + k) % 8) * 2 + y_lo}

    def xy_id(k):
        q = (m + k) % 8
        return {"dp": dp, "vocab": (q // 2) * 16 + z * 2 + q % 2}

    def remote(src, dst, ss, rs, dev):
        return pltpu.make_async_remote_copy(
            src_ref=src, dst_ref=dst, send_sem=ss, recv_sem=rs, device_id=dev, device_id_type=MESH
        )

    head_copy = pltpu.make_async_copy(head_ref, head_v, loc_sem.at[0])
    head_copy.start()
    own_copy = pltpu.make_async_copy(
        hid_ref.at[:, pl.ds(pl.multiple_of(dp * DEPTH, DEPTH), DEPTH)], spread.at[dp], loc_sem.at[1]
    )
    own_copy.start()

    barrier = pltpu.get_barrier_semaphore()
    for k in range(1, 4):
        pl.semaphore_signal(barrier, inc=1, device_id=dp_id((dp + k) % 4), device_id_type=MESH)
    for k in range(1, 8):
        pl.semaphore_signal(barrier, inc=1, device_id=z_id(k), device_id_type=MESH)
        pl.semaphore_signal(barrier, inc=1, device_id=xy_id(k), device_id_type=MESH)
    pl.semaphore_wait(barrier, 17)

    hs = []
    for k in (2, 1, 3):
        d = (dp + k) % 4
        c = remote(
            hid_ref.at[:, pl.ds(pl.multiple_of(d * DEPTH, DEPTH), DEPTH)], spread.at[dp],
            hs_s.at[k - 1], hs_r.at[k - 1], dp_id(d),
        )
        c.start()
        hs.append(c)

    lens = [len_ref[s] for s in range(8)]
    pick = (slot_of(lens, iota((ROWS, 1), 0)) == iota((ROWS, SLOTS), 1)).astype(F32).astype(BF16)
    base = 128 * core + 64 * y_hi
    my_slot = slot_of(lens, base + iota((64, 1), 0))
    my_mask = my_slot == iota((64, SLOTS), 1)
    tok = jnp.sum(jnp.where(my_mask, tok_ref[...], 0), axis=1, keepdims=True)
    old = jnp.sum(jnp.where(my_mask, old_ref[...], 0.0), axis=1, keepdims=True)
    adv = jnp.sum(jnp.where(my_mask, adv_ref[...], 0.0), axis=1, keepdims=True)

    own_copy.wait()
    for c in hs:
        c.wait()

    def compact(t, _):
        cols = pl.ds(pl.multiple_of(t * 256, 256), 256)
        full = spread[:, :, cols].reshape(SLOTS, 256)
        comp[:, cols] = jnp.dot(pick, full, preferred_element_type=F32).astype(BF16)
        return 0

    lax.fori_loop(0, DEPTH // 256, compact, 0)
    comp_copy = pltpu.make_async_copy(comp, comp_out, out_sem.at[0])
    comp_copy.start()
    head_copy.wait()

    def core_copy(j):
        return remote(
            lp.at[j, pl.ds(pl.multiple_of(128 * (1 - core), 128), 128)], rxc.at[j],
            lc_s.at[j], lc_r.at[j], dp_id(y_hi * 2 + 1 - core),
        )

    def y_copy(j):
        return remote(sy.at[j], ryy.at[j], ly_s.at[j], ly_r.at[j], dp_id((1 - y_hi) * 2 + core))

    def product(j, _):
        cols = pl.ds(pl.multiple_of(j * CC, CC), CC)
        lp[j] = jnp.dot(comp[...], head_v[:, cols], preferred_element_type=F32)
        core_copy(j).start()
        return 0

    lax.fori_loop(0, NC, product, 0)

    def chip_sum(j, _):
        core_copy(j).wait()
        far = 64 * (1 - y_hi)
        near = 64 * y_hi
        far_rows = pl.ds(pl.multiple_of(far, 64), 64)
        sy[j] = lp[j, pl.ds(pl.multiple_of(128 * core + far, 64), 64)] + rxc[j, far_rows]
        y_copy(j).start()
        cols = pl.ds(pl.multiple_of(j * CC, CC), CC)
        near_rows = pl.ds(pl.multiple_of(near, 64), 64)
        logit[:, cols] = lp[j, pl.ds(pl.multiple_of(128 * core + near, 64), 64)] + rxc[j, near_rows]
        return 0

    lax.fori_loop(0, NC, chip_sum, 0)

    def full_sum(j, _):
        y_copy(j).wait()
        cols = pl.ds(pl.multiple_of(j * CC, CC), CC)
        logit[:, cols] += ryy[j]
        return 0

    lax.fori_loop(0, NC, full_sum, 0)

    eye = iota((64, 128), 0) == iota((64, 128), 1)

    def to_row(col):
        return jnp.sum(jnp.where(eye, col, 0.0), axis=0, keepdims=True)

    def to_col(row):
        return jnp.sum(jnp.where(eye, row, 0.0), axis=1, keepdims=True)

    l = logit[...]
    hit = iota((64, COLS), 1) == tok - v * COLS
    top = jnp.max(l, axis=1, keepdims=True)
    e = jnp.exp(l - top)
    st1[...] = jnp.concatenate(
        [
            to_row(top),
            to_row(jnp.sum(e, axis=1, keepdims=True)),
            to_row(jnp.sum(e * l, axis=1, keepdims=True)),
            to_row(jnp.sum(jnp.where(hit, l, 0.0), axis=1, keepdims=True)),
            jnp.zeros((4, 128), F32),
        ],
        axis=0,
    )

    def z_copy(k):
        return remote(st1, stz.at[k - 1], z_s.at[k - 1], z_r.at[k - 1], z_id(k))

    def xy_copy(k):
        return remote(st2, stxy.at[k - 1], xy_s.at[k - 1], xy_r.at[k - 1], xy_id(k))

    for k in range(1, 8):
        z_copy(k).start()
    for k in range(1, 8):
        z_copy(k).wait()
    st2[...] = jnp.concatenate(
        list(merge([st1[...]] + [stz[k] for k in range(7)])) + [jnp.zeros((4, 128), F32)], axis=0
    )
    for k in range(1, 8):
        xy_copy(k).start()
    for k in range(1, 8):
        xy_copy(k).wait()
    top, total, weighted, target = merge([st2[...]] + [stxy[k] for k in range(7)])
    lse_row = top + jnp.log(total)
    lse = to_col(lse_row)
    entropy = to_col(lse_row - weighted / total)
    log_ratio = to_col(target) - lse - old
    slope = (kl_weight - adv) * jnp.exp(log_ratio) - kl_weight
    l = logit[...]
    shifted = l - lse
    probs = jnp.exp(shifted)
    grad = slope * (hit.astype(F32) - probs) + entropy_weight * probs * (shifted + entropy)
    mine = pl.ds(pl.multiple_of(base, 64), 64)
    dl_all[mine, :] = grad.astype(BF16)
    lane = iota((64, 128), 1)
    sm_all[mine, :] = jnp.where(lane == 0, log_ratio, jnp.where(lane == 1, entropy, 0.0))

    far = pl.ds(pl.multiple_of(128 * core + 64 * (1 - y_hi), 64), 64)
    y_dev, c_dev = dp_id((1 - y_hi) * 2 + core), dp_id(y_hi * 2 + 1 - core)
    dy = remote(dl_all.at[mine], dl_all.at[mine], d_s.at[0], d_r.at[0], y_dev)
    dc = remote(dl_all.at[mine], dl_all.at[mine], d_s.at[1], d_r.at[1], c_dev)
    dyc = remote(dl_all.at[far], dl_all.at[far], d_s.at[2], d_r.at[2], c_dev)
    dy.start()
    dc.start()
    sm = []
    for k in range(1, 4):
        c = remote(sm_all.at[mine], sm_all.at[mine], m_s.at[k - 1], m_r.at[k - 1], dp_id((dp + k) % 4))
        c.start()
        sm.append(c)
    dy.wait_recv()
    dyc.start()
    dc.wait_recv()
    dyc.wait_recv()
    dl_copy = pltpu.make_async_copy(dl_all, dl_out, out_sem.at[1])
    dl_copy.start()

    row_slot = slot_of(lens, iota((1, ROWS), 1))
    r = iota((SLOTS, 1), 0)
    slot_xy = (r // 128) * 128 + ((r // 8) % 8) * 16 + ((r // 64) % 2) * 8 + r % 8
    slot_z = ((r // 16) % 4) * 128 + (r // 64) * 16 + ((r // 8) % 2) * 8 + r % 8
    me_first = {True: m, False: z}
    id_first = {True: xy_id, False: z_id}
    me_second = {True: z, False: m}
    id_second = {True: z_id, False: xy_id}

    def first_copy(t, k, xy):
        q = (me_first[xy] + k) % 8
        return remote(
            part.at[t, pl.ds(pl.multiple_of(q * 64, 64), 64)], rx1.at[t, k - 1],
            a_s.at[t, k - 1], a_r.at[t, k - 1], id_first[xy](k),
        )

    def second_copy(t, k, xy):
        q = (me_second[xy] + k) % 8
        return remote(
            s2.at[t, pl.ds(pl.multiple_of(q * 16, 16), 16)], rx2.at[t, k - 1],
            b_s.at[t, k - 1], b_r.at[t, k - 1], id_second[xy](k),
        )

    def expand(slots):
        put = (slots == row_slot).astype(F32).astype(BF16)

        def step(j, _):
            cols = pl.ds(pl.multiple_of(j * CC, CC), CC)
            dle[:, cols] = jnp.dot(put, dl_all[:, cols], preferred_element_type=F32).astype(BF16)
            return 0

        lax.fori_loop(0, NC, step, 0)

    def partial(t, xy):
        def step(h, _):
            rows = pl.ds(pl.multiple_of(t * TF + h * 256, 256), 256)
            cols = pl.ds(pl.multiple_of(h * 256, 256), 256)
            part[t, :, cols] = lax.dot_general(
                dle[...], head_v[rows, :], (((1,), (1,)), ((), ())), preferred_element_type=F32
            ).astype(BF16)
            return 0

        lax.fori_loop(0, TF // 256, step, 0)

        def send(k, _):
            first_copy(t, k, xy).start()
            return 0

        lax.fori_loop(1, 8, send, 0)

    order = [(t, t in TILES_XY) for t in range(NT)]
    order = [o for o in order if not o[1]] + [o for o in order if o[1]]
    done = None
    for t, xy in order:
        if done is not xy:
            expand(slot_xy if xy else slot_z)
            done = xy
        partial(t, xy)

    for c in sm:
        c.wait()
    mask = slot_of(lens, iota((ROWS, 1), 0)) == dp * GROUP + iota((ROWS, GROUP), 1)
    vals = sm_all[...]
    lr_out[...] = jnp.sum(jnp.where(mask, vals[:, 0:1], 0.0), axis=0, keepdims=True)
    en_out[...] = jnp.sum(jnp.where(mask, vals[:, 1:2], 0.0), axis=0, keepdims=True)

    for t, xy in order:
        def wait_first(k, _, t=t, xy=xy):
            first_copy(t, k, xy).wait()
            return 0

        lax.fori_loop(1, 8, wait_first, 0)
        acc = part[t, pl.ds(pl.multiple_of(me_first[xy] * 64, 64), 64)].astype(F32)
        for k in range(7):
            acc = acc + rx1[t, k].astype(F32)
        for q in range(8):
            rows = acc[8 * q : 8 * q + 8]
            s2[t, 16 * q : 16 * q + 16] = jnp.concatenate([rows[:, 0:256], rows[:, 256:512]], axis=0).astype(BF16)

        def send_second(k, _, t=t, xy=xy):
            second_copy(t, k, xy).start()
            return 0

        lax.fori_loop(1, 8, send_second, 0)

    for t, xy in order:
        def wait_second(k, _, t=t, xy=xy):
            second_copy(t, k, xy).wait()
            return 0

        lax.fori_loop(1, 8, wait_second, 0)
        acc = s2[t, pl.ds(pl.multiple_of(me_second[xy] * 16, 16), 16)].astype(F32)
        for k in range(7):
            acc = acc + rx2[t, k].astype(F32)
        gh_acc[:, t * TF : t * TF + 256] = acc[0:8]
        gh_acc[:, t * TF + 256 : t * TF + 512] = acc[8:16]
    gh_out[...] = gh_acc[...]
    dy.wait_send()
    dc.wait_send()
    dyc.wait_send()
    comp_copy.wait()
    dl_copy.wait()


def head_kernel(comp_ref, dl_ref, lr_ref, en_ref, gh_ref, gw_out, lr_out, en_out, gh_out):
    gw_out[...] = lax.dot_general(
        comp_ref[...], dl_ref[...], (((0,), (0,)), ((), ())), preferred_element_type=F32
    ).astype(BF16)
    lr_out[...] = lr_ref[...]
    en_out[...] = en_ref[...]
    gh_out[...] = gh_ref[...].astype(BF16)


def local(hidden, head, token_ids, old_logp, advantages, lengths):
    vmem = pl.BlockSpec(memory_space=pltpu.VMEM)
    hbm = pl.BlockSpec(memory_space=pl.ANY)
    dma = pltpu.SemaphoreType.DMA
    comp, dl, lr, en, gh = pl.pallas_call(
        main_kernel,
        out_shape=(
            jax.ShapeDtypeStruct((ROWS, DEPTH), BF16),
            jax.ShapeDtypeStruct((ROWS, COLS), BF16),
            jax.ShapeDtypeStruct((1, GROUP), F32),
            jax.ShapeDtypeStruct((1, GROUP), F32),
            jax.ShapeDtypeStruct((8, DEPTH), F32),
        ),
        in_specs=[pl.BlockSpec(memory_space=pltpu.SMEM), vmem, vmem, vmem, hbm, hbm],
        out_specs=(hbm, hbm, vmem, vmem, vmem),
        scratch_shapes=[
            pltpu.VMEM((4, GROUP, DEPTH), BF16),
            pltpu.VMEM((DEPTH, COLS), BF16),
            pltpu.VMEM((ROWS, DEPTH), BF16),
            pltpu.VMEM((NC, ROWS, CC), F32),
            pltpu.VMEM((NC, 128, CC), F32),
            pltpu.VMEM((NC, 64, CC), F32),
            pltpu.VMEM((NC, 64, CC), F32),
            pltpu.VMEM((64, COLS), F32),
            pltpu.VMEM((8, 128), F32),
            pltpu.VMEM((8, 128), F32),
            pltpu.VMEM((7, 8, 128), F32),
            pltpu.VMEM((7, 8, 128), F32),
            pltpu.VMEM((ROWS, COLS), BF16),
            pltpu.VMEM((ROWS, 128), F32),
            pltpu.VMEM((SLOTS, COLS), BF16),
            pltpu.VMEM((NT, SLOTS, TF), BF16),
            pltpu.VMEM((NT, 7, 64, TF), BF16),
            pltpu.VMEM((NT, 128, 256), BF16),
            pltpu.VMEM((NT, 7, 16, 256), BF16),
            pltpu.VMEM((8, DEPTH), F32),
            dma((2,)), dma((3,)), dma((3,)), dma((NC,)), dma((NC,)), dma((NC,)), dma((NC,)),
            dma((7,)), dma((7,)), dma((7,)), dma((7,)), dma((3,)), dma((3,)), dma((3,)), dma((3,)),
            dma((NT, 7)), dma((NT, 7)), dma((NT, 7)), dma((NT, 7)), dma((2,)),
        ],
        compiler_params=pltpu.CompilerParams(
            collective_id=0, has_side_effects=True, vmem_limit_bytes=48 * 1024 * 1024
        ),
        name="main",
    )(lengths, token_ids[None], old_logp[None], advantages[None], hidden, head)
    whole = lambda shape: pl.BlockSpec(shape, lambda i: (0, 0))
    gw, lr, en, gh = pl.pallas_call(
        head_kernel,
        grid=(DEPTH // 256,),
        out_shape=(
            jax.ShapeDtypeStruct((DEPTH, COLS), BF16),
            jax.ShapeDtypeStruct((1, GROUP), F32),
            jax.ShapeDtypeStruct((1, GROUP), F32),
            jax.ShapeDtypeStruct((8, DEPTH), BF16),
        ),
        in_specs=[
            pl.BlockSpec((ROWS, 256), lambda i: (0, i)), whole((ROWS, COLS)), whole((1, GROUP)), whole((1, GROUP)),
            whole((8, DEPTH)),
        ],
        out_specs=(pl.BlockSpec((256, COLS), lambda i: (i, 0)), whole((1, GROUP)), whole((1, GROUP)), whole((8, DEPTH))),
        compiler_params=pltpu.CompilerParams(vmem_limit_bytes=32 * 1024 * 1024),
        name="head_grad",
    )(comp, dl, lr, en, gh)
    return lr[0], en[0], gh, gw


def solution(mesh):
    in_specs = (P("dp", None), P("dp", "vocab"), P(), P(), P(), P())
    out_specs = (P("dp"), P("dp"), P("vocab", "dp"), P("dp", "vocab"))
    return jax.shard_map(local, mesh=mesh, in_specs=in_specs, out_specs=out_specs, check_vma=False)
```

time: 772 us -> 106 us (0.14)
  waiting for transfers between devices: 362 us -> 0 us
  blocking collectives: 342 us -> 0 us
  Pallas kernels: 0 us -> 100 us
  matrix products: 20 us -> 0 us
  local copies, waits for them, and re-layouts: 21.6 us -> 4.28 us
  between operations: 13.9 us -> 0.65 us
    reduce_scatter x2 -> x0, waiting for transfers between devices: 345 us -> none  [the longest x1 303 us: local(): lax.psum_scatter(part, 'vocab', scatter_dimension=0, tiled=True)]
    psum x1 -> x0, blocking collectives: 157 us -> none  [local(): lax.psum((jnp.sum(scaled, axis=1), jnp.sum(scaled * logits, axis=1), targ...]
    pmax x1 -> x0, blocking collectives: 154 us -> none  [local(): top = lax.pmax(local_top, 'vocab')]
    pallas_call x0 -> x2, Pallas kernels: none -> 100 us  [the longest x1 94.7 us: local(): pl.pallas_call(main_kernel, out_shape=(jax.ShapeDtypeStruct((ROWS, DEPTH)...]
    all_to_all x1 -> x0, blocking collectives: 30.8 us -> none  [local(): lax.all_to_all(hidden, 'dp', split_axis=1, concat_axis=0, tiled=True)]
    dot_general x3 -> x0, matrix products: 20 us -> none  [the longest x1 7.81 us: local(): lax.dot_general(piece, head, (((1,), (1,)), ((), ())), preferred_element_...]
    all_gather x1 -> x0, waiting for transfers between devices: 16.8 us -> none  [local(): piece = lax.all_gather(dlogits, 'dp', axis=0, tiled=True)]
    unnamed x14 -> x10, local copies, waits for them, and re-layouts: 13.9 us -> 4.28 us
  transfers between devices with their start and end apart: 3 -> 0, of which waited for: 3 -> 0; matrix products, arithmetic and copies ran while one was open for 2% -> 0% of each run, Pallas kernels for 0% -> 0%
where the time goes in v1:
time: 106 us; the launch traced here: 105 us
  Pallas kernels  100 us (94%)
  local copies, waits for them, and re-layouts  4.28 us (4%)
    pallas_call x1, Pallas kernels, local(): pl.pallas_call(main_kernel, out_shape=(jax.ShapeDtypeStruct((ROWS, DEPTH)...  94.7 us
    pallas_call x1, Pallas kernels, local(): pl.pallas_call(head_kernel, grid=(DEPTH // 256,), out_shape=(jax.ShapeDty...  5.4 us
    unnamed x10, local copies, waits for them, and re-layouts  4.28 us

profile of v1, /device:TPU:8, one launch (start us, length us, event | category | flops | bytes accessed | tf_op | source)
XLA Modules:
  0.0 105.0 jit_solution(13575618338615006966)
XLA Ops:
  0.6 0.0 copy-start
  0.6 1.6 %copy-done = bf16[128,8192]{1,0:T(8,128)(2,1)S(1)} copy-done((bf16[128,8192]{1,0:T(8,128)(2,1)S(1)}, bf16[128,8192]{1,0:T(8,128)(2,1)}, u32[]{:S(2)}) %copy-start) | copy-done | bytes 2097176
  2.2 0.0 copy-start.1
  2.2 0.7 copy-done.1
  2.9 0.0 copy-start.2
  2.9 0.7 copy-done.2
  3.6 0.0 copy-start.3
  3.6 0.7 copy-done.3
  4.3 0.0 copy-start.4
  4.3 0.7 copy-done.4
  4.9 94.7 %main.1 = (bf16[256,2048]{1,0:T(8,128)(2,1)S(1)}, bf16[256,1280]{1,0:T(8,128)(2,1)S(1)}, f32[1,128]{1,0:T(1,128)S(1)}, f32[1,128]{1,0:T(1,128)S(1)}, f32[8,2048]{1,0:T(8,128)S(1)}) custom-call(s32[8]{0:T(128)S(1)} %copy-done.4, s32[1,512]{1,0:T(1,128)S(1)} %bitcast.5, f32[1,512]{1,0:T(1,128)S(1)} %bitcast.6, f32[1,512]{1,0:T(1,128)S(1)} %bitcast.7, ...), custom_call_target="tpu_custom_call" | custom-call | tf_op jit(solution)/shard_map/main/pallas_call | solution.py:358
  99.6 5.4 %head_grad.1 = (bf16[2048,1280]{1,0:T(8,128)(2,1)}, f32[1,128]{1,0:T(1,128)}, f32[1,128]{1,0:T(1,128)}, bf16[8,2048]{1,0:T(8,128)(2,1)}) custom-call(bf16[256,2048]{1,0:T(8,128)(2,1)S(1)} %get-tuple-element.13.comp_ref, bf16[256,1280]{1,0:T(8,128)(2,1)S(1)} %get-tuple-element.14.dl_ref, f32[1,128]{1,0:T(1,128)S(1)} %get-tuple-element.15.lr_ref, ...), custom_call_target="tpu_custom_call" | custom-call | tf_op jit(solution)/shard_map/head_grad/pallas_call | solution.py:400
Async XLA Ops:
  0.6 1.6 %copy-start = (bf16[128,8192]{1,0:T(8,128)(2,1)S(1)}, bf16[128,8192]{1,0:T(8,128)(2,1)}, u32[]{:S(2)}) copy-start(bf16[128,8192]{1,0:T(8,128)(2,1)} %hid_ref.1) | copy-start | bytes 6291460
  2.2 0.7 copy-start.1
  2.9 0.7 copy-start.2
  3.6 0.7 copy-start.3
  4.3 0.7 copy-start.4

commit v2 on v1

v2 whole, which is shorter than its diff:
```python
import functools

import jax
import jax.numpy as jnp
from jax import lax
from jax.experimental import pallas as pl
from jax.experimental.pallas import tpu as pltpu
from jax.sharding import PartitionSpec as P

kl_weight = 0.2
entropy_weight = 0.1

F32 = jnp.float32
BF16 = jnp.bfloat16
MESH = pl.DeviceIdType.MESH

RESP = 64
SLOTS = 512
ROWS = 256
GROUP = 128
DEPTH = 2048
COLS = 1280
CC = 256
NC = COLS // CC
TF = 512
NT = DEPTH // TF
XF = 1408
ZF = DEPTH - XF


def iota(shape, dim):
    return lax.broadcasted_iota(jnp.int32, shape, dim)


def merge(parts):
    top = functools.reduce(jnp.maximum, [p[0:1] for p in parts])
    scales = [jnp.exp(p[0:1] - top) for p in parts]
    total = sum(p[1:2] * s for p, s in zip(parts, scales))
    weighted = sum(p[2:3] * s for p, s in zip(parts, scales))
    target = sum(p[3:4] for p in parts)
    return top, total, weighted, target


def plan(lens):
    ends = [0]
    for z in range(8):
        for x in range(4):
            count = jnp.clip(lens[2 * x + z // 4] - 16 * (z % 4), 0, 16)
            ends.append(ends[-1] + count)
    return ends


def rank_of(lens, ends, slot):
    seq, pos = slot // RESP, slot % RESP
    block = ((seq % 2) * 4 + pos // 16) * 4 + seq // 2
    first = jnp.zeros_like(slot)
    for b in range(1, 32):
        first = jnp.where(block == b, ends[b], first)
    length = jnp.zeros_like(slot)
    for s in range(8):
        length = jnp.where(seq == s, lens[s], length)
    return jnp.where(pos < length, first + pos % 16, -1)


def row_of(rank):
    return jnp.where(rank >= 0, (rank % 8) * 32 + rank // 8, -1)


def onehot(mask):
    return mask.astype(F32).astype(BF16)


def main_kernel(
    len_hbm, tok_hbm, old_hbm, adv_hbm, hid_ref, head_ref,
    turn_out, dl_out, lr_out, en_out, gh_out,
    len_ref, tok_ref, old_ref, adv_ref,
    spread, head_v, comp, lp, rxc, sy, ryy, logit, st1, st2, stz, stxy, dl_all, sm_all, part, rx1, s2, rx2, gat, turned,
    loc_sem, hc_s, hc_r, hx_s, hx_r, hz_s, hz_r, fx_s, fx_r, fz_s, fz_r,
    lc_s, lc_r, ly_s, ly_r, z_s, z_r, xy_s, xy_r, d_s, d_r, m_s, m_r, a_s, a_r, b_s, b_r, g_s, g_r, out_sem,
):
    dp = lax.axis_index("dp")
    v = lax.axis_index("vocab")
    y_hi, core = dp // 2, dp % 2
    x, z, y_lo = v // 16, (v // 2) % 8, v % 2
    m = x * 2 + y_lo

    def dp_id(d):
        return {"dp": d, "vocab": v}

    def z_id(k):
        return {"dp": dp, "vocab": x * 16 + ((z + k) % 8) * 2 + y_lo}

    def xy_id(k):
        q = (m + k) % 8
        return {"dp": dp, "vocab": (q // 2) * 16 + z * 2 + q % 2}

    def remote(src, dst, ss, rs, dev):
        return pltpu.make_async_remote_copy(
            src_ref=src, dst_ref=dst, send_sem=ss, recv_sem=rs, device_id=dev, device_id_type=MESH
        )

    small = [
        pltpu.make_async_copy(a, b, loc_sem.at[2 + i])
        for i, (a, b) in enumerate(((len_hbm, len_ref), (tok_hbm, tok_ref), (old_hbm, old_ref), (adv_hbm, adv_ref)))
    ]
    for c in small:
        c.start()

    barrier = pltpu.get_barrier_semaphore()
    for k in range(1, 4):
        pl.semaphore_signal(barrier, inc=1, device_id=dp_id((dp + k) % 4), device_id_type=MESH)
    for k in range(1, 8):
        pl.semaphore_signal(barrier, inc=1, device_id=z_id(k), device_id_type=MESH)
        pl.semaphore_signal(barrier, inc=1, device_id=xy_id(k), device_id_type=MESH)
    own_copy = pltpu.make_async_copy(
        hid_ref.at[:, pl.ds(pl.multiple_of(dp * DEPTH, DEPTH), DEPTH)], spread.at[dp], loc_sem.at[1]
    )
    own_copy.start()
    head_copy = pltpu.make_async_copy(head_ref, head_v, loc_sem.at[0])
    head_copy.start()
    pl.semaphore_wait(barrier, 17)

    z_rows = pl.ds(pl.multiple_of(16 * z, 16), 16)
    x_rows = pl.ds(pl.multiple_of(32 * x, 32), 32)
    z_cols, x_cols = pl.ds(XF, ZF), pl.ds(0, XF)

    def cross_z(c):
        d = (1 - y_hi) * 2 + c
        src = hid_ref.at[z_rows, pl.ds(pl.multiple_of(d * DEPTH + XF, 128), ZF)]
        return remote(src, spread.at[dp, z_rows, z_cols], hz_s.at[c], hz_r.at[core], dp_id(d))

    def cross_x(c):
        d = (1 - y_hi) * 2 + c
        src = hid_ref.at[x_rows, pl.ds(pl.multiple_of(d * DEPTH, 128), XF)]
        return remote(src, spread.at[dp, x_rows, x_cols], hx_s.at[c], hx_r.at[core], dp_id(d))

    def near_core():
        d = y_hi * 2 + 1 - core
        src = hid_ref.at[:, pl.ds(pl.multiple_of(d * DEPTH, DEPTH), DEPTH)]
        return remote(src, spread.at[dp], hc_s.at[0], hc_r.at[0], dp_id(d))

    def pass_z(g, k):
        ref = spread.at[(1 - y_hi) * 2 + g, z_rows, z_cols]
        return remote(ref, ref, fz_s.at[g, k - 1], fz_r.at[g, k - 1], z_id(k))

    def pass_x(g, k):
        ref = spread.at[(1 - y_hi) * 2 + g, x_rows, x_cols]
        return remote(ref, ref, fx_s.at[g, k - 1], fx_r.at[g, k - 1], xy_id(2 * k))

    for c in (0, 1):
        cross_z(c).start()
        cross_x(c).start()
    near_core().start()

    for g in (0, 1):
        ref = spread.at[(1 - y_hi) * 2 + g, z_rows, z_cols]
        remote(ref, ref, hz_s.at[g], hz_r.at[g], z_id(1)).wait_recv()
        for k in range(1, 8):
            pass_z(g, k).start()
        ref = spread.at[(1 - y_hi) * 2 + g, x_rows, x_cols]
        remote(ref, ref, hx_s.at[g], hx_r.at[g], z_id(1)).wait_recv()
        for k in range(1, 4):
            pass_x(g, k).start()

    for c in small:
        c.wait()
    lens = [len_ref[s] for s in range(8)]
    ends = plan(lens)
    pick = onehot(row_of(rank_of(lens, ends, iota((1, SLOTS), 1))) == iota((ROWS, SLOTS), 0))
    base = 128 * y_hi + 64 * core
    my_mask = row_of(rank_of(lens, ends, iota((1, SLOTS), 1))) == base + iota((64, SLOTS), 0)
    tok = jnp.sum(jnp.where(my_mask, tok_ref[...], 0), axis=1, keepdims=True)
    old = jnp.sum(jnp.where(my_mask, old_ref[...], 0.0), axis=1, keepdims=True)
    adv = jnp.sum(jnp.where(my_mask, adv_ref[...], 0.0), axis=1, keepdims=True)

    own_copy.wait()
    near_core().wait()
    for g in (0, 1):
        cross_z(g).wait_send()
        cross_x(g).wait_send()
        for k in range(1, 8):
            pass_z(g, k).wait()
        for k in range(1, 4):
            pass_x(g, k).wait()

    def compact(t, _):
        cols = pl.ds(pl.multiple_of(t * 256, 256), 256)
        full = spread[:, :, cols].reshape(SLOTS, 256)
        comp[:, cols] = jnp.dot(pick, full, preferred_element_type=F32).astype(BF16)
        return 0

    lax.fori_loop(0, DEPTH // 256, compact, 0)
    head_copy.wait()

    def core_copy(j):
        return remote(
            lp.at[j, :, 1 - core], rxc.at[j],
            lc_s.at[j], lc_r.at[j], dp_id(y_hi * 2 + 1 - core),
        )

    def y_copy(j):
        return remote(sy.at[j], ryy.at[j], ly_s.at[j], ly_r.at[j], dp_id((1 - y_hi) * 2 + core))

    def product(j, _):
        cols = pl.ds(pl.multiple_of(j * CC, CC), CC)
        lp[j] = jnp.dot(comp[...], head_v[:, cols], preferred_element_type=F32).reshape(2, 2, 64, CC)
        core_copy(j).start()
        return 0

    lax.fori_loop(0, NC, product, 0)

    def chip_sum(j, _):
        core_copy(j).wait()
        sy[j] = lp[j, 1 - y_hi, core] + rxc[j, 1 - y_hi]
        y_copy(j).start()
        cols = pl.ds(pl.multiple_of(j * CC, CC), CC)
        logit[:, cols] = lp[j, y_hi, core] + rxc[j, y_hi]
        return 0

    lax.fori_loop(0, NC, chip_sum, 0)

    def full_sum(j, _):
        y_copy(j).wait()
        cols = pl.ds(pl.multiple_of(j * CC, CC), CC)
        logit[:, cols] += ryy[j]
        return 0

    lax.fori_loop(0, NC, full_sum, 0)

    eye = iota((64, 128), 0) == iota((64, 128), 1)

    def to_row(col):
        return jnp.sum(jnp.where(eye, col, 0.0), axis=0, keepdims=True)

    def to_col(row):
        return jnp.sum(jnp.where(eye, row, 0.0), axis=1, keepdims=True)

    l = logit[...]
    hit = iota((64, COLS), 1) == tok - v * COLS
    top = jnp.max(l, axis=1, keepdims=True)
    e = jnp.exp(l - top)
    st1[...] = jnp.concatenate(
        [
            to_row(top),
            to_row(jnp.sum(e, axis=1, keepdims=True)),
            to_row(jnp.sum(e * l, axis=1, keepdims=True)),
            to_row(jnp.sum(jnp.where(hit, l, 0.0), axis=1, keepdims=True)),
            jnp.zeros((4, 128), F32),
        ],
        axis=0,
    )

    def z_copy(k):
        return remote(st1, stz.at[k - 1], z_s.at[k - 1], z_r.at[k - 1], z_id(k))

    def xy_copy(k):
        return remote(st2, stxy.at[k - 1], xy_s.at[k - 1], xy_r.at[k - 1], xy_id(k))

    for k in range(1, 8):
        z_copy(k).start()

    def turn(t, _):
        cols = pl.ds(pl.multiple_of(t * 256, 256), 256)
        turned[cols, :] = comp[:, cols].astype(F32).T.astype(BF16)
        return 0

    lax.fori_loop(0, DEPTH // 256, turn, 0)
    turn_copy = pltpu.make_async_copy(turned, turn_out, out_sem.at[1])
    turn_copy.start()
    for k in range(1, 8):
        z_copy(k).wait()
    st2[...] = jnp.concatenate(
        list(merge([st1[...]] + [stz[k] for k in range(7)])) + [jnp.zeros((4, 128), F32)], axis=0
    )
    for k in range(1, 8):
        xy_copy(k).start()
    for k in range(1, 8):
        xy_copy(k).wait()
    top, total, weighted, target = merge([st2[...]] + [stxy[k] for k in range(7)])
    lse_row = top + jnp.log(total)
    lse = to_col(lse_row)
    entropy = to_col(lse_row - weighted / total)
    log_ratio = to_col(target) - lse - old
    slope = (kl_weight - adv) * jnp.exp(log_ratio) - kl_weight
    l = logit[...]
    shifted = l - lse
    probs = jnp.exp(shifted)
    grad = slope * (hit.astype(F32) - probs) + entropy_weight * probs * (shifted + entropy)
    mine = pl.ds(pl.multiple_of(base, 64), 64)
    dl_all[mine, :] = grad.astype(BF16)

    far = pl.ds(pl.multiple_of(128 * (1 - y_hi) + 64 * core, 64), 64)
    y_dev, c_dev = dp_id((1 - y_hi) * 2 + core), dp_id(y_hi * 2 + 1 - core)
    dy = remote(dl_all.at[mine], dl_all.at[mine], d_s.at[0], d_r.at[0], y_dev)
    dc = remote(dl_all.at[mine], dl_all.at[mine], d_s.at[1], d_r.at[1], c_dev)
    dyc = remote(dl_all.at[far], dl_all.at[far], d_s.at[2], d_r.at[2], c_dev)
    dy.start()
    dc.start()
    lane = iota((64, 128), 1)
    sm_all[mine, :] = jnp.where(lane == 0, log_ratio, jnp.where(lane == 1, entropy, 0.0))
    sm = []
    for k in range(1, 4):
        c = remote(sm_all.at[mine], sm_all.at[mine], m_s.at[k - 1], m_r.at[k - 1], dp_id((dp + k) % 4))
        c.start()
        sm.append(c)

    def first_copy(t, q):
        return remote(
            part.at[t, pl.ds(pl.multiple_of(q * 32, 32), 32)], rx1.at[t, (q - m) % 8 - 1],
            a_s.at[t, q], a_r.at[t, (q - m) % 8 - 1], xy_id((q - m) % 8),
        )

    def partial(half):
        rows = pl.ds(pl.multiple_of(128 * half, 128), 128)

        def step(t, _):
            for h in range(TF // 256):
                feats = pl.ds(pl.multiple_of(t * TF + h * 256, 256), 256)
                part[t, rows, h * 256 : h * 256 + 256] = lax.dot_general(
                    dl_all[rows, :], head_v[feats, :], (((1,), (1,)), ((), ())), preferred_element_type=F32
                ).astype(BF16)
            for i in range(4):
                q = half * 4 + i

                @pl.when(q != m)
                def _():
                    first_copy(t, q).start()

            return 0

        lax.fori_loop(0, NT, step, 0)

    dc.wait_recv()
    partial(y_hi)
    dy.wait_recv()
    dyc.start()
    dyc.wait_recv()
    partial(1 - y_hi)
    dl_copy = pltpu.make_async_copy(dl_all, dl_out, out_sem.at[0])
    dl_copy.start()

    for c in sm:
        c.wait()
    mask = row_of(rank_of(lens, ends, dp * GROUP + iota((1, GROUP), 1))) == iota((ROWS, GROUP), 0)
    vals = sm_all[...]
    lr_out[...] = jnp.sum(jnp.where(mask, vals[:, 0:1], 0.0), axis=0, keepdims=True)
    en_out[...] = jnp.sum(jnp.where(mask, vals[:, 1:2], 0.0), axis=0, keepdims=True)

    def first_row(z_of, member):
        start = jnp.zeros_like(z_of)
        end = jnp.full_like(z_of, ends[4])
        for q in range(1, 8):
            start = jnp.where(z_of == q, ends[4 * q], start)
            end = jnp.where(z_of == q, ends[4 * q + 4], end)
        return (start - member + 7) // 8, end

    col = iota((128, 1), 0)
    start, end = first_row(col // 16, m)
    row = start + col % 8
    row = jnp.where(row * 8 + m < end, row, -1)
    row = row + 32 * ((col // 8) % 2) * (row >= 0).astype(jnp.int32)
    deal = onehot(row == iota((128, 64), 1))

    def second_copy(t, k):
        q = (z + k) % 8
        return remote(
            s2.at[t, pl.ds(pl.multiple_of(q * 16, 16), 16)], rx2.at[t, k - 1],
            b_s.at[t, k - 1], b_r.at[t, k - 1], z_id(k),
        )

    def third_copy(t, k):
        return remote(gat.at[t, 0], gat.at[t, k], g_s.at[t, k - 1], g_r.at[t, k - 1], xy_id(k))

    def first_sum(t, _):
        def wait(k, _):
            remote(rx1.at[t, k], rx1.at[t, k], a_s.at[t, 0], a_r.at[t, k], xy_id(1)).wait_recv()
            return 0

        lax.fori_loop(0, 7, wait, 0)
        acc = part[t, pl.ds(pl.multiple_of(m * 32, 32), 32)].astype(F32)
        for k in range(7):
            acc = acc + rx1[t, k].astype(F32)
        both = jnp.concatenate([acc[:, 0:256], acc[:, 256:512]], axis=0).astype(BF16)
        s2[t] = jnp.dot(deal, both, preferred_element_type=F32).astype(BF16)

        def send(k, _):
            second_copy(t, k).start()
            return 0

        lax.fori_loop(1, 8, send, 0)
        return 0

    lax.fori_loop(0, NT, first_sum, 0)

    def second_sum(t, _):
        def wait(k, _):
            second_copy(t, k).wait()
            return 0

        lax.fori_loop(1, 8, wait, 0)
        acc = s2[t, pl.ds(pl.multiple_of(z * 16, 16), 16)].astype(F32)
        for k in range(7):
            acc = acc + rx2[t, k].astype(F32)
        gat[t, 0] = acc.astype(BF16)

        def send(k, _):
            third_copy(t, k).start()
            return 0

        lax.fori_loop(1, 8, send, 0)
        return 0

    lax.fori_loop(0, NT, second_sum, 0)

    side = iota((16, 1), 0)
    rank = rank_of(lens, ends, 128 * x + 16 * z + 8 * y_lo + side % 8)
    owner = rank % 8
    start, _ = first_row(jnp.zeros_like(owner) + z, owner)
    place = ((m - owner) % 8) * 16 + (side // 8) * 8 + rank // 8 - start
    place = jnp.where(rank >= 0, place, -1)
    take = onehot(place == iota((16, 128), 1))
    for t in range(NT):
        def wait_third(k, _, t=t):
            third_copy(t, k).wait()
            return 0

        lax.fori_loop(1, 8, wait_third, 0)
        rows = jnp.dot(take, gat[t].reshape(128, 256), preferred_element_type=F32)
        gh_out[:, t * TF : t * TF + 256] = rows[0:8]
        gh_out[:, t * TF + 256 : t * TF + 512] = rows[8:16]

    def drain(t, _):
        def one(q, _):
            @pl.when(q != m)
            def _():
                first_copy(t, q).wait_send()

            return 0

        lax.fori_loop(0, 8, one, 0)
        return 0

    lax.fori_loop(0, NT, drain, 0)
    dy.wait_send()
    dc.wait_send()
    dyc.wait_send()
    dl_copy.wait()
    turn_copy.wait()


def head_kernel(turned_ref, dl_ref, lr_ref, en_ref, gh_ref, gw_out, lr_out, en_out, gh_out):
    gw_out[...] = jnp.dot(turned_ref[...], dl_ref[...], preferred_element_type=F32).astype(BF16)
    lr_out[...] = lr_ref[...]
    en_out[...] = en_ref[...]
    gh_out[...] = gh_ref[...].astype(BF16)


def local(hidden, head, token_ids, old_logp, advantages, lengths):
    vmem = pl.BlockSpec(memory_space=pltpu.VMEM)
    hbm = pl.BlockSpec(memory_space=pltpu.HBM)
    dma = pltpu.SemaphoreType.DMA
    turned, dl, lr, en, gh = pl.pallas_call(
        main_kernel,
        out_shape=(
            jax.ShapeDtypeStruct((DEPTH, ROWS), BF16),
            jax.ShapeDtypeStruct((ROWS, COLS), BF16),
            jax.ShapeDtypeStruct((1, GROUP), F32),
            jax.ShapeDtypeStruct((1, GROUP), F32),
            jax.ShapeDtypeStruct((8, DEPTH), F32),
        ),
        in_specs=[hbm] * 6,
        out_specs=(hbm, hbm, vmem, vmem, vmem),
        scratch_shapes=[
            pltpu.SMEM((8,), jnp.int32),
            pltpu.VMEM((1, SLOTS), jnp.int32),
            pltpu.VMEM((1, SLOTS), F32),
            pltpu.VMEM((1, SLOTS), F32),
            pltpu.VMEM((4, GROUP, DEPTH), BF16),
            pltpu.VMEM((DEPTH, COLS), BF16),
            pltpu.VMEM((ROWS, DEPTH), BF16),
            pltpu.VMEM((NC, 2, 2, 64, CC), F32),
            pltpu.VMEM((NC, 2, 64, CC), F32),
            pltpu.VMEM((NC, 64, CC), F32),
            pltpu.VMEM((NC, 64, CC), F32),
            pltpu.VMEM((64, COLS), F32),
            pltpu.VMEM((8, 128), F32),
            pltpu.VMEM((8, 128), F32),
            pltpu.VMEM((7, 8, 128), F32),
            pltpu.VMEM((7, 8, 128), F32),
            pltpu.VMEM((ROWS, COLS), BF16),
            pltpu.VMEM((ROWS, 128), F32),
            pltpu.VMEM((NT, ROWS, TF), BF16),
            pltpu.VMEM((NT, 7, 32, TF), BF16),
            pltpu.VMEM((NT, 128, 256), BF16),
            pltpu.VMEM((NT, 7, 16, 256), BF16),
            pltpu.VMEM((NT, 8, 16, 256), BF16),
            pltpu.VMEM((DEPTH, ROWS), BF16),
            dma((6,)), dma((1,)), dma((1,)), dma((2,)), dma((2,)), dma((2,)), dma((2,)),
            dma((2, 3)), dma((2, 3)), dma((2, 7)), dma((2, 7)),
            dma((NC,)), dma((NC,)), dma((NC,)), dma((NC,)),
            dma((7,)), dma((7,)), dma((7,)), dma((7,)), dma((3,)), dma((3,)), dma((3,)), dma((3,)),
            dma((NT, 8)), dma((NT, 7)), dma((NT, 7)), dma((NT, 7)), dma((NT, 7)), dma((NT, 7)), dma((2,)),
        ],
        compiler_params=pltpu.CompilerParams(
            collective_id=0, has_side_effects=True, vmem_limit_bytes=62 * 1024 * 1024
        ),
        name="main",
    )(lengths, token_ids[None], old_logp[None], advantages[None], hidden, head)
    whole = lambda shape: pl.BlockSpec(shape, lambda i: (0, 0))
    gw, lr, en, gh = pl.pallas_call(
        head_kernel,
        grid=(DEPTH // 256,),
        out_shape=(
            jax.ShapeDtypeStruct((DEPTH, COLS), BF16),
            jax.ShapeDtypeStruct((1, GROUP), F32),
            jax.ShapeDtypeStruct((1, GROUP), F32),
            jax.ShapeDtypeStruct((8, DEPTH), BF16),
        ),
        in_specs=[
            pl.BlockSpec((256, ROWS), lambda i: (i, 0)), whole((ROWS, COLS)), whole((1, GROUP)), whole((1, GROUP)),
            whole((8, DEPTH)),
        ],
        out_specs=(pl.BlockSpec((256, COLS), lambda i: (i, 0)), whole((1, GROUP)), whole((1, GROUP)), whole((8, DEPTH))),
        compiler_params=pltpu.CompilerParams(vmem_limit_bytes=62 * 1024 * 1024),
        name="head_grad",
    )(turned, dl, lr, en, gh)
    return lr[0], en[0], gh, gw


def solution(mesh):
    in_specs = (P("dp", None), P("dp", "vocab"), P(), P(), P(), P())
    out_specs = (P("dp"), P("dp"), P("vocab", "dp"), P("dp", "vocab"))
    return jax.shard_map(local, mesh=mesh, in_specs=in_specs, out_specs=out_specs, check_vma=False)
```

time: 106 us -> 97.3 us (0.918)
  local copies, waits for them, and re-layouts: 4.28 us -> 0 us
  Pallas kernels: 100 us -> 95.8 us
    pallas_call x1, Pallas kernels: 94.7 us -> 88.4 us  [local(): pl.pallas_call(main_kernel, out_shape=(jax.ShapeDtypeStruct((DEPTH, ROWS)...]
    unnamed x10 -> x0, local copies, waits for them, and re-layouts: 4.28 us -> none
    pallas_call x1, Pallas kernels: 5.4 us -> 7.49 us  [local(): pl.pallas_call(head_kernel, grid=(DEPTH // 256,), out_shape=(jax.ShapeDty...]
where the time goes in v2:
time: 97.3 us; the launch traced here: 96.5 us
  Pallas kernels  95.8 us (98%)
    pallas_call x1, Pallas kernels, local(): pl.pallas_call(main_kernel, out_shape=(jax.ShapeDtypeStruct((DEPTH, ROWS)...  88.4 us
    pallas_call x1, Pallas kernels, local(): pl.pallas_call(head_kernel, grid=(DEPTH // 256,), out_shape=(jax.ShapeDty...  7.49 us

profile of v2, /device:TPU:8, one launch (start us, length us, event | category | flops | bytes accessed | tf_op | source)
XLA Modules:
  0.0 96.5 jit_solution(7394321446156244515)
XLA Ops:
  0.6 88.4 %main.1 = (bf16[2048,256]{1,0:T(8,128)(2,1)}, bf16[256,1280]{1,0:T(8,128)(2,1)}, f32[1,128]{1,0:T(1,128)}, f32[1,128]{1,0:T(1,128)}, f32[8,2048]{1,0:T(8,128)}) custom-call(s32[8]{0:T(128)} %len_hbm.1, s32[1,512]{1,0:T(1,128)} %bitcast.5, f32[1,512]{1,0:T(1,128)} %bitcast.6, f32[1,512]{1,0:T(1,128)} %bitcast.7, bf16[128,8192]{1,0:T(8,128)(2,1)} %hid_ref.1, ...), custom_call_target="tpu_custom_call" | custom-call | tf_op jit(solution)/shard_map/main/pallas_call | solution.py:462
  89.0 7.5 %head_grad.1 = (bf16[2048,1280]{1,0:T(8,128)(2,1)}, f32[1,128]{1,0:T(1,128)}, f32[1,128]{1,0:T(1,128)}, bf16[8,2048]{1,0:T(8,128)(2,1)}) custom-call(bf16[2048,256]{1,0:T(8,128)(2,1)} %get-tuple-element.13.turned_ref, bf16[256,1280]{1,0:T(8,128)(2,1)} %get-tuple-element.14.dl_ref, f32[1,128]{1,0:T(1,128)} %get-tuple-element.15.lr_ref, ...), custom_call_target="tpu_custom_call" | custom-call | tf_op jit(solution)/shard_map/head_grad/pallas_call | solution.py:510

commit v3 on v2

v3 whole, which is shorter than its diff:
```python
import functools

import jax
import jax.numpy as jnp
from jax import lax
from jax.experimental import pallas as pl
from jax.experimental.pallas import tpu as pltpu
from jax.sharding import PartitionSpec as P

kl_weight = 0.2
entropy_weight = 0.1

F32 = jnp.float32
BF16 = jnp.bfloat16
MESH = pl.DeviceIdType.MESH

RESP = 64
SLOTS = 512
ROWS = 256
GROUP = 128
DEPTH = 2048
COLS = 1280
CC = 256
NC = COLS // CC
TF = 512
NT = DEPTH // TF
XF = 1408
ZF = DEPTH - XF


def iota(shape, dim):
    return lax.broadcasted_iota(jnp.int32, shape, dim)


def merge(parts):
    top = functools.reduce(jnp.maximum, [p[0:1] for p in parts])
    scales = [jnp.exp(p[0:1] - top) for p in parts]
    total = sum(p[1:2] * s for p, s in zip(parts, scales))
    weighted = sum(p[2:3] * s for p, s in zip(parts, scales))
    target = sum(p[3:4] for p in parts)
    return top, total, weighted, target


def plan_z(lens):
    ends = [0]
    for z in range(8):
        for x in range(4):
            ends.append(ends[-1] + jnp.clip(lens[2 * x + z // 4] - 16 * (z % 4), 0, 16))
    return ends


def plan_xy(lens):
    ends = [0]
    for m in range(8):
        for i in range(8):
            ends.append(ends[-1] + jnp.clip(lens[2 * (m // 2) + i // 4] - 16 * (i % 4) - 8 * (m % 2), 0, 8))
    return ends


def rank_of(lens, ends, slot, by_z):
    seq, pos = slot // RESP, slot % RESP
    if by_z:
        block, size = ((seq % 2) * 4 + pos // 16) * 4 + seq // 2, 16
    else:
        block, size = ((seq // 2) * 2 + (pos // 8) % 2) * 8 + (seq % 2) * 4 + pos // 16, 8
    first = jnp.zeros_like(slot)
    for b in range(1, len(ends) - 1):
        first = jnp.where(block == b, ends[b], first)
    length = jnp.zeros_like(slot)
    for s in range(8):
        length = jnp.where(seq == s, lens[s], length)
    return jnp.where(pos < length, first + pos % size, -1)


def row_of(rank):
    return jnp.where(rank >= 0, (rank % 8) * 32 + rank // 8, -1)


def onehot(mask):
    return mask.astype(F32).astype(BF16)


def main_kernel(
    len_hbm, tok_hbm, old_hbm, adv_hbm, hid_ref, head_ref,
    turn_out, dl_out, lr_out, en_out, gh_out,
    len_ref, tok_ref, old_ref, adv_ref,
    spread, head_v, comp, lp, rxc, sy, ryy, logit, lg, st1, st2, st3, stz, stxy, dl_all, dl_z, part, rx1, s2, rx2, gat, turned,
    loc_sem, hc_s, hc_r, hx_s, hx_r, hz_s, hz_r, fx_s, fx_r, fz_s, fz_r,
    lc_s, lc_r, ly_s, ly_r, z_s, z_r, xy_s, xy_r, gc_s, gc_r, gy_s, gy_r, gf_s, gf_r, m_s, m_r, a_s, a_r, b_s, b_r, g_s, g_r, out_sem,
):
    dp = lax.axis_index("dp")
    v = lax.axis_index("vocab")
    y_hi, core = dp // 2, dp % 2
    x, z, y_lo = v // 16, (v // 2) % 8, v % 2
    m = x * 2 + y_lo

    def dp_id(d):
        return {"dp": d, "vocab": v}

    def z_id(k):
        return {"dp": dp, "vocab": x * 16 + ((z + k) % 8) * 2 + y_lo}

    def xy_id(k):
        q = (m + k) % 8
        return {"dp": dp, "vocab": (q // 2) * 16 + z * 2 + q % 2}

    def remote(src, dst, ss, rs, dev):
        return pltpu.make_async_remote_copy(
            src_ref=src, dst_ref=dst, send_sem=ss, recv_sem=rs, device_id=dev, device_id_type=MESH
        )

    small = [
        pltpu.make_async_copy(a, b, loc_sem.at[2 + i])
        for i, (a, b) in enumerate(((len_hbm, len_ref), (tok_hbm, tok_ref), (old_hbm, old_ref), (adv_hbm, adv_ref)))
    ]
    for c in small:
        c.start()

    barrier = pltpu.get_barrier_semaphore()
    for k in range(1, 4):
        pl.semaphore_signal(barrier, inc=1, device_id=dp_id((dp + k) % 4), device_id_type=MESH)
    for k in range(1, 8):
        pl.semaphore_signal(barrier, inc=1, device_id=z_id(k), device_id_type=MESH)
        pl.semaphore_signal(barrier, inc=1, device_id=xy_id(k), device_id_type=MESH)
    own_copy = pltpu.make_async_copy(
        hid_ref.at[:, pl.ds(pl.multiple_of(dp * DEPTH, DEPTH), DEPTH)], spread.at[dp], loc_sem.at[1]
    )
    own_copy.start()
    head_copy = pltpu.make_async_copy(head_ref, head_v, loc_sem.at[0])
    head_copy.start()
    pl.semaphore_wait(barrier, 17)

    z_rows = pl.ds(pl.multiple_of(16 * z, 16), 16)
    x_rows = pl.ds(pl.multiple_of(32 * x, 32), 32)
    z_cols, x_cols = pl.ds(XF, ZF), pl.ds(0, XF)

    def cross_z(c):
        d = (1 - y_hi) * 2 + c
        src = hid_ref.at[z_rows, pl.ds(pl.multiple_of(d * DEPTH + XF, 128), ZF)]
        return remote(src, spread.at[dp, z_rows, z_cols], hz_s.at[c], hz_r.at[core], dp_id(d))

    def cross_x(c):
        d = (1 - y_hi) * 2 + c
        src = hid_ref.at[x_rows, pl.ds(pl.multiple_of(d * DEPTH, 128), XF)]
        return remote(src, spread.at[dp, x_rows, x_cols], hx_s.at[c], hx_r.at[core], dp_id(d))

    def near_core():
        d = y_hi * 2 + 1 - core
        src = hid_ref.at[:, pl.ds(pl.multiple_of(d * DEPTH, DEPTH), DEPTH)]
        return remote(src, spread.at[dp], hc_s.at[0], hc_r.at[0], dp_id(d))

    def pass_z(g, k):
        ref = spread.at[(1 - y_hi) * 2 + g, z_rows, z_cols]
        return remote(ref, ref, fz_s.at[g, k - 1], fz_r.at[g, k - 1], z_id(k))

    def pass_x(g, k):
        ref = spread.at[(1 - y_hi) * 2 + g, x_rows, x_cols]
        return remote(ref, ref, fx_s.at[g, k - 1], fx_r.at[g, k - 1], xy_id(2 * k))

    for c in (0, 1):
        cross_z(c).start()
        cross_x(c).start()
    near_core().start()

    for g in (0, 1):
        ref = spread.at[(1 - y_hi) * 2 + g, z_rows, z_cols]
        remote(ref, ref, hz_s.at[g], hz_r.at[g], z_id(1)).wait_recv()
        for k in range(1, 8):
            pass_z(g, k).start()
        ref = spread.at[(1 - y_hi) * 2 + g, x_rows, x_cols]
        remote(ref, ref, hx_s.at[g], hx_r.at[g], z_id(1)).wait_recv()
        for k in range(1, 4):
            pass_x(g, k).start()

    for c in small:
        c.wait()
    lens = [len_ref[s] for s in range(8)]
    ends_z, ends_xy = plan_z(lens), plan_xy(lens)
    slots = iota((1, SLOTS), 1)
    row_z = row_of(rank_of(lens, ends_z, slots, True))
    hits = row_z == iota((ROWS, SLOTS), 0)
    pick = onehot(hits)
    pick_xy = onehot(row_of(rank_of(lens, ends_xy, slots, False)) == iota((ROWS, SLOTS), 0))
    turn_order = lax.dot_general(pick_xy, pick, (((1,), (1,)), ((), ())), preferred_element_type=F32).astype(BF16)
    tok = jnp.sum(jnp.where(hits, tok_ref[...], 0), axis=1, keepdims=True)
    base = 128 * y_hi + 64 * core
    my_mask = row_z == base + iota((64, SLOTS), 0)
    my_tok = jnp.sum(jnp.where(my_mask, tok_ref[...], 0), axis=1, keepdims=True)
    old = jnp.sum(jnp.where(my_mask, old_ref[...], 0.0), axis=1, keepdims=True)
    adv = jnp.sum(jnp.where(my_mask, adv_ref[...], 0.0), axis=1, keepdims=True)

    own_copy.wait()
    near_core().wait()

    def compact(half, first):
        mine = onehot(row_of(rank_of(lens, ends_z, half * 256 + iota((1, 256), 1), True)) == iota((ROWS, 256), 0))

        def step(t, _):
            cols = pl.ds(pl.multiple_of(t * 256, 256), 256)
            full = spread[pl.ds(2 * half, 2), :, cols].reshape(256, 256)
            rows = jnp.dot(mine, full, preferred_element_type=F32).astype(BF16)
            comp[:, cols] = rows if first else comp[:, cols] + rows
            return 0

        lax.fori_loop(0, DEPTH // 256, step, 0)

    compact(y_hi, True)
    for g in (0, 1):
        cross_z(g).wait_send()
        cross_x(g).wait_send()
        for k in range(1, 8):
            pass_z(g, k).wait()
        for k in range(1, 4):
            pass_x(g, k).wait()
    compact(1 - y_hi, False)
    head_copy.wait()

    def core_copy(j):
        return remote(
            lp.at[j, :, 1 - core], rxc.at[j],
            lc_s.at[j], lc_r.at[j], dp_id(y_hi * 2 + 1 - core),
        )

    def y_copy(j):
        return remote(sy.at[j], ryy.at[j], ly_s.at[j], ly_r.at[j], dp_id((1 - y_hi) * 2 + core))

    def chip_sum(j):
        core_copy(j).wait()
        sy[j] = lp[j, 1 - y_hi, core] + rxc[j, 1 - y_hi]
        y_copy(j).start()
        cols = pl.ds(pl.multiple_of(j * CC, CC), CC)
        logit[:, cols] = lp[j, y_hi, core] + rxc[j, y_hi]

    def product(j, _):
        cols = pl.ds(pl.multiple_of(j * CC, CC), CC)
        lp[j] = jnp.dot(comp[...], head_v[:, cols], preferred_element_type=F32).reshape(2, 2, 64, CC)
        core_copy(j).start()

        @pl.when(j > 0)
        def _():
            chip_sum(j - 1)

        return 0

    lax.fori_loop(0, NC, product, 0)
    chip_sum(NC - 1)

    y_dev, c_dev = dp_id((1 - y_hi) * 2 + core), dp_id(y_hi * 2 + 1 - core)

    def give(j, sems, dev, side):
        ref = lg.at[j, side, core]
        return remote(ref, ref, sems[0].at[j], sems[1].at[j], dev)

    def full_sum(j, _):
        y_copy(j).wait()
        cols = pl.ds(pl.multiple_of(j * CC, CC), CC)
        l = logit[:, cols] + ryy[j]
        logit[:, cols] = l
        lg[j, y_hi, core] = l
        give(j, (gy_s, gy_r), y_dev, y_hi).start()
        give(j, (gc_s, gc_r), c_dev, y_hi).start()
        return 0

    lax.fori_loop(0, NC, full_sum, 0)

    eye = iota((64, 128), 0) == iota((64, 128), 1)

    def to_row(col):
        return jnp.sum(jnp.where(eye, col, 0.0), axis=0, keepdims=True)

    def to_col(row):
        return jnp.sum(jnp.where(eye, row, 0.0), axis=1, keepdims=True)

    l = logit[...]
    hit = iota((64, COLS), 1) == my_tok - v * COLS
    top = jnp.max(l, axis=1, keepdims=True)
    e = jnp.exp(l - top)
    st1[...] = jnp.concatenate(
        [
            to_row(top),
            to_row(jnp.sum(e, axis=1, keepdims=True)),
            to_row(jnp.sum(e * l, axis=1, keepdims=True)),
            to_row(jnp.sum(jnp.where(hit, l, 0.0), axis=1, keepdims=True)),
            jnp.zeros((4, 128), F32),
        ],
        axis=0,
    )

    def z_copy(k):
        return remote(st1, stz.at[k - 1], z_s.at[k - 1], z_r.at[k - 1], z_id(k))

    def xy_copy(k):
        return remote(st2, stxy.at[k - 1], xy_s.at[k - 1], xy_r.at[k - 1], xy_id(k))

    for k in range(1, 8):
        z_copy(k).start()

    def turn(t, _):
        cols = pl.ds(pl.multiple_of(t * 256, 256), 256)
        turned[cols, :] = comp[:, cols].astype(F32).T.astype(BF16)
        return 0

    lax.fori_loop(0, DEPTH // 256, turn, 0)
    turn_copy = pltpu.make_async_copy(turned, turn_out, out_sem.at[1])
    turn_copy.start()
    for k in range(1, 8):
        z_copy(k).wait()
    st2[...] = jnp.concatenate(
        list(merge([st1[...]] + [stz[k] for k in range(7)])) + [jnp.zeros((4, 128), F32)], axis=0
    )
    for k in range(1, 8):
        xy_copy(k).start()

    def forward(j, _):
        give(j, (gy_s, gy_r), y_dev, 1 - y_hi).wait_recv()
        give(j, (gf_s, gf_r), c_dev, 1 - y_hi).start()
        return 0

    lax.fori_loop(0, NC, forward, 0)
    for k in range(1, 8):
        xy_copy(k).wait()
    top, total, weighted, target = merge([st2[...]] + [stxy[k] for k in range(7)])
    lse_row = top + jnp.log(total)
    entropy_row = lse_row - weighted / total
    ratio_row = target - lse_row - to_row(old)
    slope_row = (kl_weight - to_row(adv)) * jnp.exp(ratio_row) - kl_weight
    st3[0] = jnp.concatenate([lse_row, entropy_row, ratio_row, slope_row, jnp.zeros((4, 128), F32)], axis=0)

    def row_copy(k):
        return remote(st3.at[0], st3.at[k], m_s.at[k - 1], m_r.at[k - 1], dp_id((dp + k) % 4))

    for k in range(1, 4):
        row_copy(k).start()

    def arrive(j, _):
        give(j, (gc_s, gc_r), c_dev, y_hi).wait()
        give(j, (gf_s, gf_r), c_dev, 1 - y_hi).wait()
        give(j, (gy_s, gy_r), y_dev, y_hi).wait_send()
        return 0

    lax.fori_loop(0, NC, arrive, 0)
    for k in range(1, 4):
        row_copy(k).wait()

    lse, entropy, log_ratio, slope = [
        jnp.concatenate([to_col(st3[(dp - d) % 4][i : i + 1]) for d in range(4)], axis=0) for i in range(4)
    ]

    def gradient(j, _):
        l = lg[j].reshape(ROWS, CC)
        hit = iota((ROWS, CC), 1) == tok - (v * COLS + j * CC)
        shifted = l - lse
        probs = jnp.exp(shifted)
        grad = slope * (hit.astype(F32) - probs) + entropy_weight * probs * (shifted + entropy)
        dl_all[:, pl.ds(pl.multiple_of(j * CC, CC), CC)] = grad.astype(BF16)
        return 0

    lax.fori_loop(0, NC, gradient, 0)
    dl_copy = pltpu.make_async_copy(dl_all, dl_out, out_sem.at[0])
    dl_copy.start()

    class By:
        pass

    by_xy, by_z = By(), By()
    by_xy.me, by_xy.peer, by_xy.other, by_xy.across, by_xy.rows = m, xy_id, z, z_id, dl_all
    by_z.me, by_z.peer, by_z.other, by_z.across, by_z.rows = z, z_id, m, xy_id, dl_z
    by_xy.starts = [ends_z[4 * q] for q in range(9)]
    by_z.starts = [ends_xy[8 * q] for q in range(9)]
    my_slots = 128 * x + 16 * z + 8 * y_lo + iota((16, 1), 0) % 8
    by_xy.rank = rank_of(lens, ends_z, my_slots, True)
    by_z.rank = rank_of(lens, ends_xy, my_slots, False)

    def first_copy(t, k, by):
        q = (by.me + k) % 8
        return remote(
            part.at[t, pl.ds(pl.multiple_of(q * 32, 32), 32)], rx1.at[t, k - 1],
            a_s.at[t, k - 1], a_r.at[t, k - 1], by.peer(k),
        )

    def partial(t, by):
        for h in range(TF // 256):
            part[t, :, h * 256 : h * 256 + 256] = lax.dot_general(
                by.rows[...], head_v[t * TF + h * 256 : t * TF + h * 256 + 256, :], (((1,), (1,)), ((), ())),
                preferred_element_type=F32,
            ).astype(BF16)

        def send(k, _):
            first_copy(t, k, by).start()
            return 0

        lax.fori_loop(1, 8, send, 0)

    order = [(0, by_xy), (3, by_z), (1, by_xy), (2, by_xy)]
    for t, by in order:
        if by is by_z:
            def reorder(j, _):
                cols = pl.ds(pl.multiple_of(j * CC, CC), CC)
                dl_z[:, cols] = jnp.dot(turn_order, dl_all[:, cols], preferred_element_type=F32).astype(BF16)
                return 0

            lax.fori_loop(0, NC, reorder, 0)
        partial(t, by)

    mask = row_of(rank_of(lens, ends_z, dp * GROUP + iota((1, GROUP), 1), True)) == iota((ROWS, GROUP), 0)
    lr_out[...] = jnp.sum(jnp.where(mask, log_ratio, 0.0), axis=0, keepdims=True)
    en_out[...] = jnp.sum(jnp.where(mask, entropy, 0.0), axis=0, keepdims=True)

    def first_row(by, owner, member):
        start = jnp.zeros_like(owner)
        end = jnp.zeros_like(owner) + by.starts[1]
        for q in range(1, 8):
            start = jnp.where(owner == q, by.starts[q], start)
            end = jnp.where(owner == q, by.starts[q + 1], end)
        return (start - member + 7) // 8, end

    def second_copy(t, k, by):
        q = (by.other + k) % 8
        return remote(
            s2.at[t, pl.ds(pl.multiple_of(q * 16, 16), 16)], rx2.at[t, k - 1],
            b_s.at[t, k - 1], b_r.at[t, k - 1], by.across(k),
        )

    def third_copy(t, k, by):
        return remote(gat.at[t, 0], gat.at[t, k], g_s.at[t, k - 1], g_r.at[t, k - 1], by.peer(k))

    for by in (by_xy, by_z):
        col = iota((128, 1), 0)
        start, end = first_row(by, col // 16, by.me)
        row = start + col % 8
        row = jnp.where(row * 8 + by.me < end, row, -1)
        row = row + 32 * ((col // 8) % 2) * (row >= 0).astype(jnp.int32)
        by.deal = onehot(row == iota((128, 64), 1))
        owner = by.rank % 8
        start, _ = first_row(by, jnp.zeros_like(owner) + by.other, owner)
        place = ((by.me - owner) % 8) * 16 + (iota((16, 1), 0) // 8) * 8 + by.rank // 8 - start
        by.take = onehot(jnp.where(by.rank >= 0, place, -1) == iota((16, 128), 1))

    def each(make):
        def step(k, _):
            make(k)
            return 0

        lax.fori_loop(1, 8, step, 0)

    for t, by in order:
        each(lambda k: first_copy(t, k, by).wait())
        acc = part[t, pl.ds(pl.multiple_of(by.me * 32, 32), 32)].astype(F32)
        for k in range(7):
            acc = acc + rx1[t, k].astype(F32)
        both = jnp.concatenate([acc[:, 0:256], acc[:, 256:512]], axis=0).astype(BF16)
        s2[t] = jnp.dot(by.deal, both, preferred_element_type=F32).astype(BF16)
        each(lambda k: second_copy(t, k, by).start())

    for t, by in order:
        each(lambda k: second_copy(t, k, by).wait())
        acc = s2[t, pl.ds(pl.multiple_of(by.other * 16, 16), 16)].astype(F32)
        for k in range(7):
            acc = acc + rx2[t, k].astype(F32)
        gat[t, 0] = acc.astype(BF16)
        each(lambda k: third_copy(t, k, by).start())

    for t, by in order:
        each(lambda k: third_copy(t, k, by).wait())
        rows = jnp.dot(by.take, gat[t].reshape(128, 256), preferred_element_type=F32)
        gh_out[:, t * TF : t * TF + 256] = rows[0:8]
        gh_out[:, t * TF + 256 : t * TF + 512] = rows[8:16]
    dl_copy.wait()
    turn_copy.wait()


def head_kernel(turned_hbm, dl_hbm, lr_ref, en_ref, gh_ref, gw_out, lr_out, en_out, gh_out, turned, dl, gw, in_sem, out_sem):
    lr_out[...] = lr_ref[...]
    en_out[...] = en_ref[...]
    gh_out[...] = gh_ref[...].astype(BF16)
    dl_copies = []
    for i in range(4):
        c = pltpu.make_async_copy(dl_hbm.at[pl.ds(64 * i, 64)], dl.at[pl.ds(64 * i, 64)], in_sem.at[i])
        c.start()
        dl_copies.append(c)

    def piece(ref, i):
        return ref.at[pl.ds(i * 256, 256)]

    def load(i):
        return pltpu.make_async_copy(piece(turned_hbm, i), piece(turned, i), in_sem.at[4 + i])

    def store(i):
        return pltpu.make_async_copy(piece(gw, i), piece(gw_out, i), out_sem.at[i])

    for i in range(8):
        load(i).start()
    for c in dl_copies:
        c.wait()
    for i in range(8):
        load(i).wait()
        piece(gw, i)[...] = jnp.dot(piece(turned, i)[...], dl[...], preferred_element_type=F32).astype(BF16)
        store(i).start()
    for i in range(8):
        store(i).wait()


def local(hidden, head, token_ids, old_logp, advantages, lengths):
    vmem = pl.BlockSpec(memory_space=pltpu.VMEM)
    hbm = pl.BlockSpec(memory_space=pltpu.HBM)
    dma = pltpu.SemaphoreType.DMA
    turned, dl, lr, en, gh = pl.pallas_call(
        main_kernel,
        out_shape=(
            jax.ShapeDtypeStruct((DEPTH, ROWS), BF16),
            jax.ShapeDtypeStruct((ROWS, COLS), BF16),
            jax.ShapeDtypeStruct((1, GROUP), F32),
            jax.ShapeDtypeStruct((1, GROUP), F32),
            jax.ShapeDtypeStruct((8, DEPTH), F32),
        ),
        in_specs=[hbm] * 6,
        out_specs=(hbm, hbm, vmem, vmem, vmem),
        scratch_shapes=[
            pltpu.SMEM((8,), jnp.int32),
            pltpu.VMEM((1, SLOTS), jnp.int32),
            pltpu.VMEM((1, SLOTS), F32),
            pltpu.VMEM((1, SLOTS), F32),
            pltpu.VMEM((4, GROUP, DEPTH), BF16),
            pltpu.VMEM((DEPTH, COLS), BF16),
            pltpu.VMEM((ROWS, DEPTH), BF16),
            pltpu.VMEM((NC, 2, 2, 64, CC), F32),
            pltpu.VMEM((NC, 2, 64, CC), F32),
            pltpu.VMEM((NC, 64, CC), F32),
            pltpu.VMEM((NC, 64, CC), F32),
            pltpu.VMEM((64, COLS), F32),
            pltpu.VMEM((NC, 2, 2, 64, CC), F32),
            pltpu.VMEM((8, 128), F32),
            pltpu.VMEM((8, 128), F32),
            pltpu.VMEM((4, 8, 128), F32),
            pltpu.VMEM((7, 8, 128), F32),
            pltpu.VMEM((7, 8, 128), F32),
            pltpu.VMEM((ROWS, COLS), BF16),
            pltpu.VMEM((ROWS, COLS), BF16),
            pltpu.VMEM((NT, ROWS, TF), BF16),
            pltpu.VMEM((NT, 7, 32, TF), BF16),
            pltpu.VMEM((NT, 128, 256), BF16),
            pltpu.VMEM((NT, 7, 16, 256), BF16),
            pltpu.VMEM((NT, 8, 16, 256), BF16),
            pltpu.VMEM((DEPTH, ROWS), BF16),
            dma((6,)), dma((1,)), dma((1,)), dma((2,)), dma((2,)), dma((2,)), dma((2,)),
            dma((2, 3)), dma((2, 3)), dma((2, 7)), dma((2, 7)),
            dma((NC,)), dma((NC,)), dma((NC,)), dma((NC,)),
            dma((7,)), dma((7,)), dma((7,)), dma((7,)),
            dma((NC,)), dma((NC,)), dma((NC,)), dma((NC,)), dma((NC,)), dma((NC,)), dma((3,)), dma((3,)),
            dma((NT, 7)), dma((NT, 7)), dma((NT, 7)), dma((NT, 7)), dma((NT, 7)), dma((NT, 7)), dma((2,)),
        ],
        compiler_params=pltpu.CompilerParams(
            collective_id=0, has_side_effects=True, vmem_limit_bytes=62 * 1024 * 1024
        ),
        name="main",
    )(lengths, token_ids[None], old_logp[None], advantages[None], hidden, head)
    gw, lr, en, gh = pl.pallas_call(
        head_kernel,
        out_shape=(
            jax.ShapeDtypeStruct((DEPTH, COLS), BF16),
            jax.ShapeDtypeStruct((1, GROUP), F32),
            jax.ShapeDtypeStruct((1, GROUP), F32),
            jax.ShapeDtypeStruct((8, DEPTH), BF16),
        ),
        in_specs=[hbm, hbm, vmem, vmem, vmem],
        out_specs=(hbm, vmem, vmem, vmem),
        scratch_shapes=[
            pltpu.VMEM((DEPTH, ROWS), BF16), pltpu.VMEM((ROWS, COLS), BF16), pltpu.VMEM((DEPTH, COLS), BF16),
            dma((12,)), dma((8,)),
        ],
        compiler_params=pltpu.CompilerParams(vmem_limit_bytes=62 * 1024 * 1024),
        name="head_grad",
    )(turned, dl, lr, en, gh)
    return lr[0], en[0], gh, gw


def solution(mesh):
    in_specs = (P("dp", None), P("dp", "vocab"), P(), P(), P(), P())
    out_specs = (P("dp"), P("dp"), P("vocab", "dp"), P("dp", "vocab"))
    return jax.shard_map(local, mesh=mesh, in_specs=in_specs, out_specs=out_specs, check_vma=False)
```

time: 97.3 us -> 85.9 us (0.88)
  Pallas kernels: 95.8 us -> 85.1 us
    pallas_call x1, Pallas kernels: 88.4 us -> 78.4 us  [local(): pl.pallas_call(main_kernel, out_shape=(jax.ShapeDtypeStruct((DEPTH, ROWS)...]
where the time goes in v3:
time: 85.9 us; the launch traced here: 85.7 us
  Pallas kernels  85.1 us (99%)
    pallas_call x1, Pallas kernels, local(): pl.pallas_call(main_kernel, out_shape=(jax.ShapeDtypeStruct((DEPTH, ROWS)...  78.4 us
    pallas_call x1, Pallas kernels, local(): pl.pallas_call(head_kernel, out_shape=(jax.ShapeDtypeStruct((DEPTH, COLS)...  6.71 us

profile of v3, /device:TPU:8, one launch (start us, length us, event | category | flops | bytes accessed | tf_op | source)
XLA Modules:
  0.0 85.7 jit_solution(16749463396504399819)
XLA Ops:
  0.6 78.4 %main.1 = (bf16[2048,256]{1,0:T(8,128)(2,1)}, bf16[256,1280]{1,0:T(8,128)(2,1)}, f32[1,128]{1,0:T(1,128)}, f32[1,128]{1,0:T(1,128)}, f32[8,2048]{1,0:T(8,128)}) custom-call(s32[8]{0:T(128)} %len_hbm.1, s32[1,512]{1,0:T(1,128)} %bitcast.5, f32[1,512]{1,0:T(1,128)} %bitcast.6, f32[1,512]{1,0:T(1,128)} %bitcast.7, bf16[128,8192]{1,0:T(8,128)(2,1)} %hid_ref.1, ...), custom_call_target="tpu_custom_call" | custom-call | tf_op jit(solution)/shard_map/main/pallas_call | solution.py:507
  79.0 6.7 %head_grad.1 = (bf16[2048,1280]{1,0:T(8,128)(2,1)}, f32[1,128]{1,0:T(1,128)}, f32[1,128]{1,0:T(1,128)}, bf16[8,2048]{1,0:T(8,128)(2,1)}) custom-call(bf16[2048,256]{1,0:T(8,128)(2,1)} %get-tuple-element.13.turned_hbm, bf16[256,1280]{1,0:T(8,128)(2,1)} %get-tuple-element.14.dl_hbm, f32[1,128]{1,0:T(1,128)} %get-tuple-element.15.lr_ref, ...), custom_call_target="tpu_custom_call" | custom-call | tf_op jit(solution)/shard_map/head_grad/pallas_call | solution.py:557

commit v4 on v3

--- a/solution.py
+++ b/solution.py
@@ -24,8 +24,9 @@
 NC = COLS // CC
 TF = 512
 NT = DEPTH // TF
-XF = 1408
-ZF = DEPTH - XF
+XF = 1152
+ZF = 512
+DF = DEPTH - XF - ZF
 
 
 def iota(shape, dim):
@@ -69,7 +70,7 @@
     length = jnp.zeros_like(slot)
     for s in range(8):
         length = jnp.where(seq == s, lens[s], length)
-    return jnp.where(pos < length, first + pos % size, -1)
+    return jnp.where(pos < length, first + pos % size, -1), length - pos
 
 
 def row_of(rank):
@@ -82,11 +83,11 @@
 
 def main_kernel(
     len_hbm, tok_hbm, old_hbm, adv_hbm, hid_ref, head_ref,
-    turn_out, dl_out, lr_out, en_out, gh_out,
+    turned, dl_all, lr_out, en_out, gh_out,
     len_ref, tok_ref, old_ref, adv_ref,
-    spread, head_v, comp, lp, rxc, sy, ryy, logit, lg, st1, st2, st3, stz, stxy, dl_all, dl_z, part, rx1, s2, rx2, gat, turned,
-    loc_sem, hc_s, hc_r, hx_s, hx_r, hz_s, hz_r, fx_s, fx_r, fz_s, fz_r,
-    lc_s, lc_r, ly_s, ly_r, z_s, z_r, xy_s, xy_r, gc_s, gc_r, gy_s, gy_r, gf_s, gf_r, m_s, m_r, a_s, a_r, b_s, b_r, g_s, g_r, out_sem,
+    spread, head_v, comp, lp, rxc, sy, ryy, logit, lg, st1, st2, st3, stz, stxy, dl_z, part, rx1, s2, rx2, pack, give3, get3, pick_ref, order_ref, deal_ref, take_ref,
+    loc_sem, hc_s, hc_r, hx_s, hx_r, hz_s, hz_r, hd_s, hd_r, fx_s, fx_r, fz_s, fz_r,
+    lc_s, lc_r, ly_s, ly_r, z_s, z_r, xy_s, xy_r, gc_s, gc_r, gy_s, gy_r, gf_s, gf_r, m_s, m_r, a_s, a_r, b_s, b_r, g_s, g_r,
 ):
     dp = lax.axis_index("dp")
     v = lax.axis_index("vocab")
@@ -134,15 +135,23 @@
     x_rows = pl.ds(pl.multiple_of(32 * x, 32), 32)
     z_cols, x_cols = pl.ds(XF, ZF), pl.ds(0, XF)
 
+    def cross(c, sems, rows, start, size):
+        d = (1 - y_hi) * 2 + c
+        src = hid_ref.at[rows, pl.ds(pl.multiple_of(d * DEPTH + start, 128), size)]
+        return remote(src, spread.at[dp, rows, pl.ds(start, size)], sems[0].at[c], sems[1].at[core], dp_id(d))
+
+    def cross_x(c):
+        return cross(c, (hx_s, hx_r), x_rows, 0, XF)
+
     def cross_z(c):
-        d = (1 - y_hi) * 2 + c
-        src = hid_ref.at[z_rows, pl.ds(pl.multiple_of(d * DEPTH + XF, 128), ZF)]
-        return remote(src, spread.at[dp, z_rows, z_cols], hz_s.at[c], hz_r.at[core], dp_id(d))
-
-    def cross_x(c):
-        d = (1 - y_hi) * 2 + c
-        src = hid_ref.at[x_rows, pl.ds(pl.multiple_of(d * DEPTH, 128), XF)]
-        return remote(src, spread.at[dp, x_rows, x_cols], hx_s.at[c], hx_r.at[core], dp_id(d))
+        return cross(c, (hz_s, hz_r), z_rows, XF, ZF)
+
+    def cross_d(c):
+        return cross(c, (hd_s, hd_r), pl.ds(0, GROUP), XF + ZF, DF)
+
+    def landed(g, sems, rows, start, size):
+        ref = spread.at[(1 - y_hi) * 2 + g, rows, pl.ds(start, size)]
+        return remote(ref, ref, sems[0].at[g], sems[1].at[g], z_id(1))
 
     def near_core():
         d = y_hi * 2 + 1 - core
@@ -158,30 +167,24 @@
         return remote(ref, ref, fx_s.at[g, k - 1], fx_r.at[g, k - 1], xy_id(2 * k))
 
     for c in (0, 1):
+        cross_x(c).start()
         cross_z(c).start()
-        cross_x(c).start()
     near_core().start()
-
-    for g in (0, 1):
-        ref = spread.at[(1 - y_hi) * 2 + g, z_rows, z_cols]
-        remote(ref, ref, hz_s.at[g], hz_r.at[g], z_id(1)).wait_recv()
-        for k in range(1, 8):
-            pass_z(g, k).start()
-        ref = spread.at[(1 - y_hi) * 2 + g, x_rows, x_cols]
-        remote(ref, ref, hx_s.at[g], hx_r.at[g], z_id(1)).wait_recv()
-        for k in range(1, 4):
-            pass_x(g, k).start()
+    for c in (0, 1):
+        cross_d(c).start()
 
     for c in small:
         c.wait()
     lens = [len_ref[s] for s in range(8)]
     ends_z, ends_xy = plan_z(lens), plan_xy(lens)
     slots = iota((1, SLOTS), 1)
-    row_z = row_of(rank_of(lens, ends_z, slots, True))
+    row_z = row_of(rank_of(lens, ends_z, slots, True)[0])
     hits = row_z == iota((ROWS, SLOTS), 0)
-    pick = onehot(hits)
-    pick_xy = onehot(row_of(rank_of(lens, ends_xy, slots, False)) == iota((ROWS, SLOTS), 0))
-    turn_order = lax.dot_general(pick_xy, pick, (((1,), (1,)), ((), ())), preferred_element_type=F32).astype(BF16)
+    pick_ref[...] = onehot(hits)
+    pick_xy = onehot(row_of(rank_of(lens, ends_xy, slots, False)[0]) == iota((ROWS, SLOTS), 0))
+    order_ref[...] = lax.dot_general(
+        pick_xy, pick_ref[...], (((1,), (1,)), ((), ())), preferred_element_type=F32
+    ).astype(BF16)
     tok = jnp.sum(jnp.where(hits, tok_ref[...], 0), axis=1, keepdims=True)
     base = 128 * y_hi + 64 * core
     my_mask = row_z == base + iota((64, SLOTS), 0)
@@ -189,31 +192,61 @@
     old = jnp.sum(jnp.where(my_mask, old_ref[...], 0.0), axis=1, keepdims=True)
     adv = jnp.sum(jnp.where(my_mask, adv_ref[...], 0.0), axis=1, keepdims=True)
 
+    class By:
+        pass
+
+    by_xy, by_z = By(), By()
+    by_xy.me, by_xy.peer, by_xy.other, by_xy.across = m, xy_id, z, z_id
+    by_z.me, by_z.peer, by_z.other, by_z.across = z, z_id, m, xy_id
+    by_xy.rank = lambda slot: rank_of(lens, ends_z, slot, True)
+    by_z.rank = lambda slot: rank_of(lens, ends_xy, slot, False)
+    by_xy.slot = lambda second, first: 128 * (first // 2) + 16 * second + 8 * (first % 2)
+    by_z.slot = lambda second, first: 128 * (second // 2) + 16 * first + 8 * (second % 2)
+    for i, by in enumerate((by_xy, by_z)):
+        col = iota((128, 1), 0)
+        first, left = by.rank(by.slot(col // 16, col % 8))
+        rank = first + (by.me - first) % 8
+        row = rank // 8 + 32 * ((col // 8) % 2)
+        row = jnp.where((first >= 0) & (rank < first + jnp.minimum(left, 8)), row, -1)
+        deal_ref[i] = onehot(row == iota((128, 64), 1))
+        rank, _ = by.rank(by.slot(by.other, by.me) + col // 16)
+        place = ((by.me - rank) % 8) * 16 + col % 16
+        take_ref[i] = onehot(jnp.where(rank >= 0, place, -1) == iota((128, 128), 1))
+
+    for g in (0, 1):
+        landed(g, (hx_s, hx_r), x_rows, 0, XF).wait_recv()
+        for k in range(1, 4):
+            pass_x(g, k).start()
+        landed(g, (hz_s, hz_r), z_rows, XF, ZF).wait_recv()
+        for k in range(1, 8):
+            pass_z(g, k).start()
+
     own_copy.wait()
     near_core().wait()
 
     def compact(half, first):
-        mine = onehot(row_of(rank_of(lens, ends_z, half * 256 + iota((1, 256), 1), True)) == iota((ROWS, 256), 0))
-
         def step(t, _):
-            cols = pl.ds(pl.multiple_of(t * 256, 256), 256)
-            full = spread[pl.ds(2 * half, 2), :, cols].reshape(256, 256)
+            cols = pl.ds(pl.multiple_of(t * 512, 512), 512)
+            full = spread[pl.ds(2 * half, 2), :, cols].reshape(256, 512)
+            mine = pick_ref[:, pl.ds(pl.multiple_of(half * 256, 256), 256)]
             rows = jnp.dot(mine, full, preferred_element_type=F32).astype(BF16)
             comp[:, cols] = rows if first else comp[:, cols] + rows
             return 0
 
-        lax.fori_loop(0, DEPTH // 256, step, 0)
+        lax.fori_loop(0, DEPTH // 512, step, 0)
 
     compact(y_hi, True)
+    head_copy.wait()
     for g in (0, 1):
         cross_z(g).wait_send()
         cross_x(g).wait_send()
+        cross_d(g).wait_send()
+        landed(g, (hd_s, hd_r), pl.ds(0, GROUP), XF + ZF, DF).wait_recv()
         for k in range(1, 8):
             pass_z(g, k).wait()
         for k in range(1, 4):
             pass_x(g, k).wait()
     compact(1 - y_hi, False)
-    head_copy.wait()
 
     def core_copy(j):
         return remote(
@@ -301,8 +334,6 @@
         return 0
 
     lax.fori_loop(0, DEPTH // 256, turn, 0)
-    turn_copy = pltpu.make_async_copy(turned, turn_out, out_sem.at[1])
-    turn_copy.start()
     for k in range(1, 8):
         z_copy(k).wait()
     st2[...] = jnp.concatenate(
@@ -356,20 +387,11 @@
         return 0
 
     lax.fori_loop(0, NC, gradient, 0)
-    dl_copy = pltpu.make_async_copy(dl_all, dl_out, out_sem.at[0])
-    dl_copy.start()
-
-    class By:
-        pass
-
-    by_xy, by_z = By(), By()
-    by_xy.me, by_xy.peer, by_xy.other, by_xy.across, by_xy.rows = m, xy_id, z, z_id, dl_all
-    by_z.me, by_z.peer, by_z.other, by_z.across, by_z.rows = z, z_id, m, xy_id, dl_z
-    by_xy.starts = [ends_z[4 * q] for q in range(9)]
-    by_z.starts = [ends_xy[8 * q] for q in range(9)]
-    my_slots = 128 * x + 16 * z + 8 * y_lo + iota((16, 1), 0) % 8
-    by_xy.rank = rank_of(lens, ends_z, my_slots, True)
-    by_z.rank = rank_of(lens, ends_xy, my_slots, False)
+
+    by_xy.rows, by_z.rows = dl_all, dl_z
+    by_xy.deal, by_xy.take, by_xy.pack, by_xy.give, by_xy.get = deal_ref.at[0], take_ref.at[0], pack.at[0], give3.at[0], get3.at[0]
+    by_z.deal, by_z.take, by_z.pack, by_z.give, by_z.get = deal_ref.at[1], take_ref.at[1], pack.at[1], give3.at[1], get3.at[1]
+    by_xy.s, by_xy.r, by_z.s, by_z.r = g_s.at[0], g_r.at[0], g_s.at[1], g_r.at[1]
 
     def first_copy(t, k, by):
         q = (by.me + k) % 8
@@ -396,23 +418,15 @@
         if by is by_z:
             def reorder(j, _):
                 cols = pl.ds(pl.multiple_of(j * CC, CC), CC)
-                dl_z[:, cols] = jnp.dot(turn_order, dl_all[:, cols], preferred_element_type=F32).astype(BF16)
+                dl_z[:, cols] = jnp.dot(order_ref[...], dl_all[:, cols], preferred_element_type=F32).astype(BF16)
                 return 0
 
             lax.fori_loop(0, NC, reorder, 0)
         partial(t, by)
 
-    mask = row_of(rank_of(lens, ends_z, dp * GROUP + iota((1, GROUP), 1), True)) == iota((ROWS, GROUP), 0)
+    mask = row_of(rank_of(lens, ends_z, dp * GROUP + iota((1, GROUP), 1), True)[0]) == iota((ROWS, GROUP), 0)
     lr_out[...] = jnp.sum(jnp.where(mask, log_ratio, 0.0), axis=0, keepdims=True)
     en_out[...] = jnp.sum(jnp.where(mask, entropy, 0.0), axis=0, keepdims=True)
-
-    def first_row(by, owner, member):
-        start = jnp.zeros_like(owner)
-        end = jnp.zeros_like(owner) + by.starts[1]
-        for q in range(1, 8):
-            start = jnp.where(owner == q, by.starts[q], start)
-            end = jnp.where(owner == q, by.starts[q + 1], end)
-        return (start - member + 7) // 8, end
 
     def second_copy(t, k, by):
         q = (by.other + k) % 8
@@ -421,20 +435,8 @@
             b_s.at[t, k - 1], b_r.at[t, k - 1], by.across(k),
         )
 
-    def third_copy(t, k, by):
-        return remote(gat.at[t, 0], gat.at[t, k], g_s.at[t, k - 1], g_r.at[t, k - 1], by.peer(k))
-
-    for by in (by_xy, by_z):
-        col = iota((128, 1), 0)
-        start, end = first_row(by, col // 16, by.me)
-        row = start + col % 8
-        row = jnp.where(row * 8 + by.me < end, row, -1)
-        row = row + 32 * ((col // 8) % 2) * (row >= 0).astype(jnp.int32)
-        by.deal = onehot(row == iota((128, 64), 1))
-        owner = by.rank % 8
-        start, _ = first_row(by, jnp.zeros_like(owner) + by.other, owner)
-        place = ((by.me - owner) % 8) * 16 + (iota((16, 1), 0) // 8) * 8 + by.rank // 8 - start
-        by.take = onehot(jnp.where(by.rank >= 0, place, -1) == iota((16, 128), 1))
+    def third_copy(k, by):
+        return remote(by.give.at[(by.me + k) % 8], by.get.at[k], by.s.at[k - 1], by.r.at[k - 1], by.peer(k))
 
     def each(make):
         def step(k, _):
@@ -449,53 +451,49 @@
         for k in range(7):
             acc = acc + rx1[t, k].astype(F32)
         both = jnp.concatenate([acc[:, 0:256], acc[:, 256:512]], axis=0).astype(BF16)
-        s2[t] = jnp.dot(by.deal, both, preferred_element_type=F32).astype(BF16)
+        s2[t] = jnp.dot(by.deal[...], both, preferred_element_type=F32).astype(BF16)
         each(lambda k: second_copy(t, k, by).start())
 
+    pack[...] = jnp.zeros_like(pack)
+    by_xy.done, by_xy.tiles, by_xy.count = 0, [], 3
+    by_z.done, by_z.tiles, by_z.count = 0, [], 1
     for t, by in order:
         each(lambda k: second_copy(t, k, by).wait())
         acc = s2[t, pl.ds(pl.multiple_of(by.other * 16, 16), 16)].astype(F32)
         for k in range(7):
             acc = acc + rx2[t, k].astype(F32)
-        gat[t, 0] = acc.astype(BF16)
-        each(lambda k: third_copy(t, k, by).start())
-
-    for t, by in order:
-        each(lambda k: third_copy(t, k, by).wait())
-        rows = jnp.dot(by.take, gat[t].reshape(128, 256), preferred_element_type=F32)
-        gh_out[:, t * TF : t * TF + 256] = rows[0:8]
-        gh_out[:, t * TF + 256 : t * TF + 512] = rows[8:16]
-    dl_copy.wait()
-    turn_copy.wait()
-
-
-def head_kernel(turned_hbm, dl_hbm, lr_ref, en_ref, gh_ref, gw_out, lr_out, en_out, gh_out, turned, dl, gw, in_sem, out_sem):
+        for h in range(2):
+            for e in range(2):
+                by.pack[:, 4 * by.done + 2 * h + e, :] = acc[8 * h : 8 * h + 8, 128 * e : 128 * e + 128]
+        by.tiles.append(t)
+        by.done += 1
+        if by.done == by.count:
+            by.give[...] = by.pack[...].astype(BF16)
+            each(lambda k: third_copy(k, by).start())
+
+    for by in (by_z, by_xy):
+        by.get[0] = by.give[by.me]
+        each(lambda k: third_copy(k, by).wait())
+        rows = jnp.dot(by.take[...], by.get[...].reshape(128, 128), preferred_element_type=F32)
+        by.pack[...] = rows.reshape(8, 16, 128)
+        for i, t in enumerate(by.tiles):
+            for c in range(4):
+                gh_out[:, t * TF + c * 128 : t * TF + c * 128 + 128] = by.pack[:, 4 * i + c, :]
+
+
+def head_kernel(turned, dl, lr_ref, en_ref, gh_ref, gw_out, lr_out, en_out, gh_out, gw, out_sem):
+    def piece(ref, i):
+        return ref.at[pl.ds(i * 256, 256)]
+
+    def store(i):
+        return pltpu.make_async_copy(piece(gw, i), piece(gw_out, i), out_sem.at[i])
+
+    for i in range(8):
+        piece(gw, i)[...] = jnp.dot(piece(turned, i)[...], dl[...], preferred_element_type=F32).astype(BF16)
+        store(i).start()
     lr_out[...] = lr_ref[...]
     en_out[...] = en_ref[...]
     gh_out[...] = gh_ref[...].astype(BF16)
-    dl_copies = []
-    for i in range(4):
-        c = pltpu.make_async_copy(dl_hbm.at[pl.ds(64 * i, 64)], dl.at[pl.ds(64 * i, 64)], in_sem.at[i])
-        c.start()
-        dl_copies.append(c)
-
-    def piece(ref, i):
-        return ref.at[pl.ds(i * 256, 256)]
-
-    def load(i):
-        return pltpu.make_async_copy(piece(turned_hbm, i), piece(turned, i), in_sem.at[4 + i])
-
-    def store(i):
-        return pltpu.make_async_copy(piece(gw, i), piece(gw_out, i), out_sem.at[i])
-
-    for i in range(8):
-        load(i).start()
-    for c in dl_copies:
-        c.wait()
-    for i in range(8):
-        load(i).wait()
-        piece(gw, i)[...] = jnp.dot(piece(turned, i)[...], dl[...], preferred_element_type=F32).astype(BF16)
-        store(i).start()
     for i in range(8):
         store(i).wait()
 
@@ -504,17 +502,18 @@
     vmem = pl.BlockSpec(memory_space=pltpu.VMEM)
     hbm = pl.BlockSpec(memory_space=pltpu.HBM)
     dma = pltpu.SemaphoreType.DMA
+    keep = pltpu.with_memory_space_constraint
     turned, dl, lr, en, gh = pl.pallas_call(
         main_kernel,
         out_shape=(
-            jax.ShapeDtypeStruct((DEPTH, ROWS), BF16),
-            jax.ShapeDtypeStruct((ROWS, COLS), BF16),
-            jax.ShapeDtypeStruct((1, GROUP), F32),
-            jax.ShapeDtypeStruct((1, GROUP), F32),
-            jax.ShapeDtypeStruct((8, DEPTH), F32),
+            pltpu.VMEM((DEPTH, ROWS), BF16),
+            pltpu.VMEM((ROWS, COLS), BF16),
+            pltpu.VMEM((1, GROUP), F32),
+            pltpu.VMEM((1, GROUP), F32),
+            pltpu.VMEM((8, DEPTH), F32),
         ),
         in_specs=[hbm] * 6,
-        out_specs=(hbm, hbm, vmem, vmem, vmem),
+        out_specs=(vmem,) * 5,
         scratch_shapes=[
             pltpu.SMEM((8,), jnp.int32),
             pltpu.VMEM((1, SLOTS), jnp.int32),
@@ -535,25 +534,29 @@
             pltpu.VMEM((7, 8, 128), F32),
             pltpu.VMEM((7, 8, 128), F32),
             pltpu.VMEM((ROWS, COLS), BF16),
-            pltpu.VMEM((ROWS, COLS), BF16),
             pltpu.VMEM((NT, ROWS, TF), BF16),
             pltpu.VMEM((NT, 7, 32, TF), BF16),
             pltpu.VMEM((NT, 128, 256), BF16),
             pltpu.VMEM((NT, 7, 16, 256), BF16),
-            pltpu.VMEM((NT, 8, 16, 256), BF16),
-            pltpu.VMEM((DEPTH, ROWS), BF16),
-            dma((6,)), dma((1,)), dma((1,)), dma((2,)), dma((2,)), dma((2,)), dma((2,)),
+            pltpu.VMEM((2, 8, 16, 128), F32),
+            pltpu.VMEM((2, 8, 16, 128), BF16),
+            pltpu.VMEM((2, 8, 16, 128), BF16),
+            pltpu.VMEM((ROWS, SLOTS), BF16),
+            pltpu.VMEM((ROWS, ROWS), BF16),
+            pltpu.VMEM((2, 128, 64), BF16),
+            pltpu.VMEM((2, 128, 128), BF16),
+            dma((6,)), dma((1,)), dma((1,)), dma((2,)), dma((2,)), dma((2,)), dma((2,)), dma((2,)), dma((2,)),
             dma((2, 3)), dma((2, 3)), dma((2, 7)), dma((2, 7)),
             dma((NC,)), dma((NC,)), dma((NC,)), dma((NC,)),
             dma((7,)), dma((7,)), dma((7,)), dma((7,)),
             dma((NC,)), dma((NC,)), dma((NC,)), dma((NC,)), dma((NC,)), dma((NC,)), dma((3,)), dma((3,)),
-            dma((NT, 7)), dma((NT, 7)), dma((NT, 7)), dma((NT, 7)), dma((NT, 7)), dma((NT, 7)), dma((2,)),
+            dma((NT, 7)), dma((NT, 7)), dma((NT, 7)), dma((NT, 7)), dma((2, 7)), dma((2, 7)),
         ],
         compiler_params=pltpu.CompilerParams(
-            collective_id=0, has_side_effects=True, vmem_limit_bytes=62 * 1024 * 1024
+            collective_id=0, has_side_effects=True, vmem_limit_bytes=48 * 1024 * 1024
         ),
         name="main",
-    )(lengths, token_ids[None], old_logp[None], advantages[None], hidden, head)
+    )(*[keep(a, pltpu.HBM) for a in (lengths, token_ids[None], old_logp[None], advantages[None], hidden, head)])
     gw, lr, en, gh = pl.pallas_call(
         head_kernel,
         out_shape=(
@@ -562,15 +565,14 @@
             jax.ShapeDtypeStruct((1, GROUP), F32),
             jax.ShapeDtypeStruct((8, DEPTH), BF16),
         ),
-        in_specs=[hbm, hbm, vmem, vmem, vmem],
+        in_specs=[vmem] * 5,
         out_specs=(hbm, vmem, vmem, vmem),
         scratch_shapes=[
-            pltpu.VMEM((DEPTH, ROWS), BF16), pltpu.VMEM((ROWS, COLS), BF16), pltpu.VMEM((DEPTH, COLS), BF16),
-            dma((12,)), dma((8,)),
+            pltpu.VMEM((DEPTH, COLS), BF16), dma((8,)),
         ],
-        compiler_params=pltpu.CompilerParams(vmem_limit_bytes=62 * 1024 * 1024),
+        compiler_params=pltpu.CompilerParams(vmem_limit_bytes=40 * 1024 * 1024),
         name="head_grad",
-    )(turned, dl, lr, en, gh)
+    )(*[keep(a, pltpu.VMEM) for a in (turned, dl, lr, en, gh)])
     return lr[0], en[0], gh, gw
 
 

time: 85.9 us -> 79.2 us (0.922)
  Pallas kernels: 85.1 us -> 78.5 us
    pallas_call x1, Pallas kernels: 6.71 us -> 3.41 us  [local(): pl.pallas_call(head_kernel, out_shape=(jax.ShapeDtypeStruct((DEPTH, COLS)...]
    pallas_call x1, Pallas kernels: 78.4 us -> 75.1 us  [local(): pl.pallas_call(main_kernel, out_shape=(pltpu.VMEM((DEPTH, ROWS), BF16), p...]
where the time goes in v4:
time: 79.2 us; the launch traced here: 79.1 us
  Pallas kernels  78.5 us (99%)
    pallas_call x1, Pallas kernels, local(): pl.pallas_call(main_kernel, out_shape=(pltpu.VMEM((DEPTH, ROWS), BF16), p...  75.1 us
    pallas_call x1, Pallas kernels, local(): pl.pallas_call(head_kernel, out_shape=(jax.ShapeDtypeStruct((DEPTH, COLS)...  3.41 us

profile of v4, /device:TPU:8, one launch (start us, length us, event | category | flops | bytes accessed | tf_op | source)
XLA Modules:
  0.0 79.1 jit_solution(3589437888217916918)
XLA Ops:
  0.6 75.1 %main.1 = (bf16[2048,256]{1,0:T(8,128)(2,1)S(1)}, bf16[256,1280]{1,0:T(8,128)(2,1)S(1)}, f32[1,128]{1,0:T(1,128)S(1)}, f32[1,128]{1,0:T(1,128)S(1)}, f32[8,2048]{1,0:T(8,128)S(1)}) custom-call(s32[8]{0:T(128)} %len_hbm.1, s32[1,512]{1,0:T(1,128)} %bitcast.5, f32[1,512]{1,0:T(1,128)} %bitcast.6, f32[1,512]{1,0:T(1,128)} %bitcast.7, ...), custom_call_target="tpu_custom_call" | custom-call | tf_op jit(solution)/shard_map/main/pallas_call | solution.py:506
  75.7 3.4 %head_grad.1 = (bf16[2048,1280]{1,0:T(8,128)(2,1)}, f32[1,128]{1,0:T(1,128)}, f32[1,128]{1,0:T(1,128)}, bf16[8,2048]{1,0:T(8,128)(2,1)}) custom-call(bf16[2048,256]{1,0:T(8,128)(2,1)S(1)} %get-tuple-element.13.turned, bf16[256,1280]{1,0:T(8,128)(2,1)S(1)} %get-tuple-element.14.dl, f32[1,128]{1,0:T(1,128)S(1)} %get-tuple-element.15.lr_ref, ...), custom_call_target="tpu_custom_call" | custom-call | tf_op jit(solution)/shard_map/head_grad/pallas_call | solution.py:560

commit v5 on v4

--- a/solution.py
+++ b/solution.py
@@ -24,9 +24,10 @@
 NC = COLS // CC
 TF = 512
 NT = DEPTH // TF
-XF = 1152
+XF = 1024
 ZF = 512
 DF = DEPTH - XF - ZF
+XH = XF // 2
 
 
 def iota(shape, dim):
@@ -83,11 +84,11 @@
 
 def main_kernel(
     len_hbm, tok_hbm, old_hbm, adv_hbm, hid_ref, head_ref,
-    turned, dl_all, lr_out, en_out, gh_out,
+    gw, lr_out, en_out, gh_out,
     len_ref, tok_ref, old_ref, adv_ref,
-    spread, head_v, comp, lp, rxc, sy, ryy, logit, lg, st1, st2, st3, stz, stxy, dl_z, part, rx1, s2, rx2, pack, give3, get3, pick_ref, order_ref, deal_ref, take_ref,
+    spread, head_v, comp, lp, rxc, sy, ryy, logit, lg, st1, st2, stz, stxy, turned, dl_all, dl_z, part, rx1, s2, rx2, pack, give3, get3, pick_ref, order_ref, deal_ref, take_ref,
     loc_sem, hc_s, hc_r, hx_s, hx_r, hz_s, hz_r, hd_s, hd_r, fx_s, fx_r, fz_s, fz_r,
-    lc_s, lc_r, ly_s, ly_r, z_s, z_r, xy_s, xy_r, gc_s, gc_r, gy_s, gy_r, gf_s, gf_r, m_s, m_r, a_s, a_r, b_s, b_r, g_s, g_r,
+    lc_s, lc_r, ly_s, ly_r, z_s, z_r, xy_s, xy_r, gc_s, gc_r, gy_s, gy_r, gf_s, gf_r, a_s, a_r, b_s, b_r, g_s, g_r,
 ):
     dp = lax.axis_index("dp")
     v = lax.axis_index("vocab")
@@ -98,12 +99,12 @@
     def dp_id(d):
         return {"dp": d, "vocab": v}
 
-    def z_id(k):
-        return {"dp": dp, "vocab": x * 16 + ((z + k) % 8) * 2 + y_lo}
-
-    def xy_id(k):
+    def z_id(k, far=False):
+        return {"dp": y_hi * 2 + 1 - core if far else dp, "vocab": x * 16 + ((z + k) % 8) * 2 + y_lo}
+
+    def xy_id(k, far=False):
         q = (m + k) % 8
-        return {"dp": dp, "vocab": (q // 2) * 16 + z * 2 + q % 2}
+        return {"dp": (1 - y_hi) * 2 + core if far else dp, "vocab": (q // 2) * 16 + z * 2 + q % 2}
 
     def remote(src, dst, ss, rs, dev):
         return pltpu.make_async_remote_copy(
@@ -121,27 +122,28 @@
     for k in range(1, 4):
         pl.semaphore_signal(barrier, inc=1, device_id=dp_id((dp + k) % 4), device_id_type=MESH)
     for k in range(1, 8):
-        pl.semaphore_signal(barrier, inc=1, device_id=z_id(k), device_id_type=MESH)
-        pl.semaphore_signal(barrier, inc=1, device_id=xy_id(k), device_id_type=MESH)
+        for far in (False, True):
+            pl.semaphore_signal(barrier, inc=1, device_id=z_id(k, far), device_id_type=MESH)
+            pl.semaphore_signal(barrier, inc=1, device_id=xy_id(k, far), device_id_type=MESH)
     own_copy = pltpu.make_async_copy(
         hid_ref.at[:, pl.ds(pl.multiple_of(dp * DEPTH, DEPTH), DEPTH)], spread.at[dp], loc_sem.at[1]
     )
     own_copy.start()
     head_copy = pltpu.make_async_copy(head_ref, head_v, loc_sem.at[0])
     head_copy.start()
-    pl.semaphore_wait(barrier, 17)
+    pl.semaphore_wait(barrier, 31)
 
     z_rows = pl.ds(pl.multiple_of(16 * z, 16), 16)
     x_rows = pl.ds(pl.multiple_of(32 * x, 32), 32)
-    z_cols, x_cols = pl.ds(XF, ZF), pl.ds(0, XF)
+    z_cols = pl.ds(XF, ZF)
 
     def cross(c, sems, rows, start, size):
         d = (1 - y_hi) * 2 + c
         src = hid_ref.at[rows, pl.ds(pl.multiple_of(d * DEPTH + start, 128), size)]
         return remote(src, spread.at[dp, rows, pl.ds(start, size)], sems[0].at[c], sems[1].at[core], dp_id(d))
 
-    def cross_x(c):
-        return cross(c, (hx_s, hx_r), x_rows, 0, XF)
+    def cross_x(c, w):
+        return cross(c, (hx_s.at[w], hx_r.at[w]), x_rows, w * XH, XH)
 
     def cross_z(c):
         return cross(c, (hz_s, hz_r), z_rows, XF, ZF)
@@ -162,13 +164,16 @@
         ref = spread.at[(1 - y_hi) * 2 + g, z_rows, z_cols]
         return remote(ref, ref, fz_s.at[g, k - 1], fz_r.at[g, k - 1], z_id(k))
 
-    def pass_x(g, k):
-        ref = spread.at[(1 - y_hi) * 2 + g, x_rows, x_cols]
-        return remote(ref, ref, fx_s.at[g, k - 1], fx_r.at[g, k - 1], xy_id(2 * k))
+    def pass_x(g, k, w):
+        ref = spread.at[(1 - y_hi) * 2 + g, x_rows, pl.ds(w * XH, XH)]
+        return remote(ref, ref, fx_s.at[w, g, k - 1], fx_r.at[w, g, k - 1], xy_id(2 * k))
 
     for c in (0, 1):
-        cross_x(c).start()
+        cross_x(c, 0).start()
+    for c in (0, 1):
         cross_z(c).start()
+    for c in (0, 1):
+        cross_x(c, 1).start()
     near_core().start()
     for c in (0, 1):
         cross_d(c).start()
@@ -189,8 +194,8 @@
     base = 128 * y_hi + 64 * core
     my_mask = row_z == base + iota((64, SLOTS), 0)
     my_tok = jnp.sum(jnp.where(my_mask, tok_ref[...], 0), axis=1, keepdims=True)
-    old = jnp.sum(jnp.where(my_mask, old_ref[...], 0.0), axis=1, keepdims=True)
-    adv = jnp.sum(jnp.where(my_mask, adv_ref[...], 0.0), axis=1, keepdims=True)
+    old = jnp.sum(jnp.where(hits, old_ref[...], 0.0), axis=1, keepdims=True)
+    adv = jnp.sum(jnp.where(hits, adv_ref[...], 0.0), axis=1, keepdims=True)
 
     class By:
         pass
@@ -213,13 +218,18 @@
         place = ((by.me - rank) % 8) * 16 + col % 16
         take_ref[i] = onehot(jnp.where(rank >= 0, place, -1) == iota((128, 128), 1))
 
+    def pass_half(w):
+        for g in (0, 1):
+            landed(g, (hx_s.at[w], hx_r.at[w]), x_rows, w * XH, XH).wait_recv()
+            for k in (2, 1, 3):
+                pass_x(g, k, w).start()
+
+    pass_half(0)
     for g in (0, 1):
-        landed(g, (hx_s, hx_r), x_rows, 0, XF).wait_recv()
-        for k in range(1, 4):
-            pass_x(g, k).start()
         landed(g, (hz_s, hz_r), z_rows, XF, ZF).wait_recv()
-        for k in range(1, 8):
+        for k in (4, 3, 5, 2, 6, 1, 7):
             pass_z(g, k).start()
+    pass_half(1)
 
     own_copy.wait()
     near_core().wait()
@@ -239,13 +249,15 @@
     head_copy.wait()
     for g in (0, 1):
         cross_z(g).wait_send()
-        cross_x(g).wait_send()
+        cross_x(g, 0).wait_send()
+        cross_x(g, 1).wait_send()
         cross_d(g).wait_send()
         landed(g, (hd_s, hd_r), pl.ds(0, GROUP), XF + ZF, DF).wait_recv()
         for k in range(1, 8):
             pass_z(g, k).wait()
         for k in range(1, 4):
-            pass_x(g, k).wait()
+            pass_x(g, k, 0).wait()
+            pass_x(g, k, 1).wait()
     compact(1 - y_hi, False)
 
     def core_copy(j):
@@ -296,13 +308,14 @@
 
     lax.fori_loop(0, NC, full_sum, 0)
 
-    eye = iota((64, 128), 0) == iota((64, 128), 1)
+    eye = iota((64, 128), 0) + 64 * core == iota((64, 128), 1)
+    eye_all = iota((128, 128), 0) == iota((128, 128), 1)
 
     def to_row(col):
         return jnp.sum(jnp.where(eye, col, 0.0), axis=0, keepdims=True)
 
     def to_col(row):
-        return jnp.sum(jnp.where(eye, row, 0.0), axis=1, keepdims=True)
+        return jnp.sum(jnp.where(eye_all, row, 0.0), axis=1, keepdims=True)
 
     l = logit[...]
     hit = iota((64, COLS), 1) == my_tok - v * COLS
@@ -310,7 +323,7 @@
     e = jnp.exp(l - top)
     st1[...] = jnp.concatenate(
         [
-            to_row(top),
+            jnp.max(jnp.where(eye, top, -1e30), axis=0, keepdims=True),
             to_row(jnp.sum(e, axis=1, keepdims=True)),
             to_row(jnp.sum(e * l, axis=1, keepdims=True)),
             to_row(jnp.sum(jnp.where(hit, l, 0.0), axis=1, keepdims=True)),
@@ -319,14 +332,16 @@
         axis=0,
     )
 
-    def z_copy(k):
-        return remote(st1, stz.at[k - 1], z_s.at[k - 1], z_r.at[k - 1], z_id(k))
-
-    def xy_copy(k):
-        return remote(st2, stxy.at[k - 1], xy_s.at[k - 1], xy_r.at[k - 1], xy_id(k))
-
-    for k in range(1, 8):
-        z_copy(k).start()
+    def z_copy(i):
+        k, far = (i + 1, False) if i < 7 else (i - 7, True)
+        return remote(st1, stz.at[i], z_s.at[i], z_r.at[i], z_id(k, far))
+
+    def xy_copy(i):
+        k, far = (i + 1, False) if i < 7 else (i - 7, True)
+        return remote(st2, stxy.at[i], xy_s.at[i], xy_r.at[i], xy_id(k, far))
+
+    for i in range(15):
+        z_copy(i).start()
 
     def turn(t, _):
         cols = pl.ds(pl.multiple_of(t * 256, 256), 256)
@@ -334,13 +349,13 @@
         return 0
 
     lax.fori_loop(0, DEPTH // 256, turn, 0)
-    for k in range(1, 8):
-        z_copy(k).wait()
+    for i in range(15):
+        z_copy(i).wait()
     st2[...] = jnp.concatenate(
-        list(merge([st1[...]] + [stz[k] for k in range(7)])) + [jnp.zeros((4, 128), F32)], axis=0
+        list(merge([st1[...]] + [stz[i] for i in range(15)])) + [jnp.zeros((4, 128), F32)], axis=0
     )
-    for k in range(1, 8):
-        xy_copy(k).start()
+    for i in range(15):
+        xy_copy(i).start()
 
     def forward(j, _):
         give(j, (gy_s, gy_r), y_dev, 1 - y_hi).wait_recv()
@@ -348,21 +363,6 @@
         return 0
 
     lax.fori_loop(0, NC, forward, 0)
-    for k in range(1, 8):
-        xy_copy(k).wait()
-    top, total, weighted, target = merge([st2[...]] + [stxy[k] for k in range(7)])
-    lse_row = top + jnp.log(total)
-    entropy_row = lse_row - weighted / total
-    ratio_row = target - lse_row - to_row(old)
-    slope_row = (kl_weight - to_row(adv)) * jnp.exp(ratio_row) - kl_weight
-    st3[0] = jnp.concatenate([lse_row, entropy_row, ratio_row, slope_row, jnp.zeros((4, 128), F32)], axis=0)
-
-    def row_copy(k):
-        return remote(st3.at[0], st3.at[k], m_s.at[k - 1], m_r.at[k - 1], dp_id((dp + k) % 4))
-
-    for k in range(1, 4):
-        row_copy(k).start()
-
     def arrive(j, _):
         give(j, (gc_s, gc_r), c_dev, y_hi).wait()
         give(j, (gf_s, gf_r), c_dev, 1 - y_hi).wait()
@@ -370,12 +370,23 @@
         return 0
 
     lax.fori_loop(0, NC, arrive, 0)
-    for k in range(1, 4):
-        row_copy(k).wait()
-
-    lse, entropy, log_ratio, slope = [
-        jnp.concatenate([to_col(st3[(dp - d) % 4][i : i + 1]) for d in range(4)], axis=0) for i in range(4)
+    for i in range(15):
+        xy_copy(i).wait()
+
+    def row_values(parts):
+        top, total, weighted, target = merge(parts)
+        lse = top + jnp.log(total)
+        return lse, lse - weighted / total, target
+
+    near_rows = row_values([st2[...]] + [stxy[i] for i in range(7)])
+    far_rows = row_values([stxy[i] for i in range(7, 15)])
+    low = y_hi == 0
+    lse, entropy, target = [
+        jnp.concatenate([to_col(jnp.where(low, a, b)), to_col(jnp.where(low, b, a))], axis=0)
+        for a, b in zip(near_rows, far_rows)
     ]
+    log_ratio = target - lse - old
+    slope = (kl_weight - adv) * jnp.exp(log_ratio) - kl_weight
 
     def gradient(j, _):
         l = lg[j].reshape(ROWS, CC)
@@ -407,11 +418,8 @@
                 preferred_element_type=F32,
             ).astype(BF16)
 
-        def send(k, _):
+        for k in range(1, 8):
             first_copy(t, k, by).start()
-            return 0
-
-        lax.fori_loop(1, 8, send, 0)
 
     order = [(0, by_xy), (3, by_z), (1, by_xy), (2, by_xy)]
     for t, by in order:
@@ -424,6 +432,13 @@
             lax.fori_loop(0, NC, reorder, 0)
         partial(t, by)
 
+    def head_part(t, _):
+        rows = pl.ds(pl.multiple_of(t * 256, 256), 256)
+        gw[rows, :] = jnp.dot(turned[rows, :], dl_all[...], preferred_element_type=F32).astype(BF16)
+        return 0
+
+    lax.fori_loop(0, DEPTH // 256, head_part, 0)
+
     mask = row_of(rank_of(lens, ends_z, dp * GROUP + iota((1, GROUP), 1), True)[0]) == iota((ROWS, GROUP), 0)
     lr_out[...] = jnp.sum(jnp.where(mask, log_ratio, 0.0), axis=0, keepdims=True)
     en_out[...] = jnp.sum(jnp.where(mask, entropy, 0.0), axis=0, keepdims=True)
@@ -439,11 +454,8 @@
         return remote(by.give.at[(by.me + k) % 8], by.get.at[k], by.s.at[k - 1], by.r.at[k - 1], by.peer(k))
 
     def each(make):
-        def step(k, _):
+        for k in range(1, 8):
             make(k)
-            return 0
-
-        lax.fori_loop(1, 8, step, 0)
 
     for t, by in order:
         each(lambda k: first_copy(t, k, by).wait())
@@ -481,21 +493,13 @@
                 gh_out[:, t * TF + c * 128 : t * TF + c * 128 + 128] = by.pack[:, 4 * i + c, :]
 
 
-def head_kernel(turned, dl, lr_ref, en_ref, gh_ref, gw_out, lr_out, en_out, gh_out, gw, out_sem):
-    def piece(ref, i):
-        return ref.at[pl.ds(i * 256, 256)]
-
-    def store(i):
-        return pltpu.make_async_copy(piece(gw, i), piece(gw_out, i), out_sem.at[i])
-
-    for i in range(8):
-        piece(gw, i)[...] = jnp.dot(piece(turned, i)[...], dl[...], preferred_element_type=F32).astype(BF16)
-        store(i).start()
+def store_kernel(gw_ref, lr_ref, en_ref, gh_ref, gw_out, lr_out, en_out, gh_out, sem):
+    copy = pltpu.make_async_copy(gw_ref, gw_out, sem.at[0])
+    copy.start()
     lr_out[...] = lr_ref[...]
     en_out[...] = en_ref[...]
     gh_out[...] = gh_ref[...].astype(BF16)
-    for i in range(8):
-        store(i).wait()
+    copy.wait()
 
 
 def local(hidden, head, token_ids, old_logp, advantages, lengths):
@@ -503,17 +507,16 @@
     hbm = pl.BlockSpec(memory_space=pltpu.HBM)
     dma = pltpu.SemaphoreType.DMA
     keep = pltpu.with_memory_space_constraint
-    turned, dl, lr, en, gh = pl.pallas_call(
+    gw, lr, en, gh = pl.pallas_call(
         main_kernel,
         out_shape=(
-            pltpu.VMEM((DEPTH, ROWS), BF16),
-            pltpu.VMEM((ROWS, COLS), BF16),
+            pltpu.VMEM((DEPTH, COLS), BF16),
             pltpu.VMEM((1, GROUP), F32),
             pltpu.VMEM((1, GROUP), F32),
             pltpu.VMEM((8, DEPTH), F32),
         ),
         in_specs=[hbm] * 6,
-        out_specs=(vmem,) * 5,
+        out_specs=(vmem,) * 4,
         scratch_shapes=[
             pltpu.SMEM((8,), jnp.int32),
             pltpu.VMEM((1, SLOTS), jnp.int32),
@@ -530,9 +533,10 @@
             pltpu.VMEM((NC, 2, 2, 64, CC), F32),
             pltpu.VMEM((8, 128), F32),
             pltpu.VMEM((8, 128), F32),
-            pltpu.VMEM((4, 8, 128), F32),
-            pltpu.VMEM((7, 8, 128), F32),
-            pltpu.VMEM((7, 8, 128), F32),
+            pltpu.VMEM((15, 8, 128), F32),
+            pltpu.VMEM((15, 8, 128), F32),
+            pltpu.VMEM((DEPTH, ROWS), BF16),
+            pltpu.VMEM((ROWS, COLS), BF16),
             pltpu.VMEM((ROWS, COLS), BF16),
             pltpu.VMEM((NT, ROWS, TF), BF16),
             pltpu.VMEM((NT, 7, 32, TF), BF16),
@@ -545,11 +549,11 @@
             pltpu.VMEM((ROWS, ROWS), BF16),
             pltpu.VMEM((2, 128, 64), BF16),
             pltpu.VMEM((2, 128, 128), BF16),
-            dma((6,)), dma((1,)), dma((1,)), dma((2,)), dma((2,)), dma((2,)), dma((2,)), dma((2,)), dma((2,)),
-            dma((2, 3)), dma((2, 3)), dma((2, 7)), dma((2, 7)),
+            dma((6,)), dma((1,)), dma((1,)), dma((2, 2)), dma((2, 2)), dma((2,)), dma((2,)), dma((2,)), dma((2,)),
+            dma((2, 2, 3)), dma((2, 2, 3)), dma((2, 7)), dma((2, 7)),
             dma((NC,)), dma((NC,)), dma((NC,)), dma((NC,)),
-            dma((7,)), dma((7,)), dma((7,)), dma((7,)),
-            dma((NC,)), dma((NC,)), dma((NC,)), dma((NC,)), dma((NC,)), dma((NC,)), dma((3,)), dma((3,)),
+            dma((15,)), dma((15,)), dma((15,)), dma((15,)),
+            dma((NC,)), dma((NC,)), dma((NC,)), dma((NC,)), dma((NC,)), dma((NC,)),
             dma((NT, 7)), dma((NT, 7)), dma((NT, 7)), dma((NT, 7)), dma((2, 7)), dma((2, 7)),
         ],
         compiler_params=pltpu.CompilerParams(
@@ -558,21 +562,19 @@
         name="main",
     )(*[keep(a, pltpu.HBM) for a in (lengths, token_ids[None], old_logp[None], advantages[None], hidden, head)])
     gw, lr, en, gh = pl.pallas_call(
-        head_kernel,
+        store_kernel,
         out_shape=(
             jax.ShapeDtypeStruct((DEPTH, COLS), BF16),
             jax.ShapeDtypeStruct((1, GROUP), F32),
             jax.ShapeDtypeStruct((1, GROUP), F32),
             jax.ShapeDtypeStruct((8, DEPTH), BF16),
         ),
-        in_specs=[vmem] * 5,
+        in_specs=[vmem] * 4,
         out_specs=(hbm, vmem, vmem, vmem),
-        scratch_shapes=[
-            pltpu.VMEM((DEPTH, COLS), BF16), dma((8,)),
-        ],
-        compiler_params=pltpu.CompilerParams(vmem_limit_bytes=40 * 1024 * 1024),
-        name="head_grad",
-    )(*[keep(a, pltpu.VMEM) for a in (turned, dl, lr, en, gh)])
+        scratch_shapes=[dma((1,))],
+        compiler_params=pltpu.CompilerParams(vmem_limit_bytes=32 * 1024 * 1024),
+        name="store",
+    )(*[keep(a, pltpu.VMEM) for a in (gw, lr, en, gh)])
     return lr[0], en[0], gh, gw
 
 

time: 79.2 us -> 74.3 us (0.938)
  Pallas kernels: 78.5 us -> 73.6 us
    pallas_call x2, Pallas kernels: 78.5 us -> 73.6 us  [the longest x1 70.6 us: local(): pl.pallas_call(main_kernel, out_shape=(pltpu.VMEM((DEPTH, COLS), BF16), p...]
where the time goes in v5:
time: 74.3 us; the launch traced here: 74.2 us
  Pallas kernels  73.6 us (99%)
    pallas_call x1, Pallas kernels, local(): pl.pallas_call(main_kernel, out_shape=(pltpu.VMEM((DEPTH, COLS), BF16), p...  70.6 us
    pallas_call x1, Pallas kernels, local(): pl.pallas_call(store_kernel, out_shape=(jax.ShapeDtypeStruct((DEPTH, COLS...  2.99 us

profile of v5, /device:TPU:8, one launch (start us, length us, event | category | flops | bytes accessed | tf_op | source)
XLA Modules:
  0.0 74.2 jit_solution(4816542152419979445)
XLA Ops:
  0.6 70.6 %main.1 = (bf16[2048,1280]{1,0:T(8,128)(2,1)S(1)}, f32[1,128]{1,0:T(1,128)S(1)}, f32[1,128]{1,0:T(1,128)S(1)}, f32[8,2048]{1,0:T(8,128)S(1)}) custom-call(s32[8]{0:T(128)} %len_hbm.1, s32[1,512]{1,0:T(1,128)} %bitcast.5, f32[1,512]{1,0:T(1,128)} %bitcast.6, f32[1,512]{1,0:T(1,128)} %bitcast.7, bf16[128,8192]{1,0:T(8,128)(2,1)} %hid_ref.1, ...), custom_call_target="tpu_custom_call" | custom-call | tf_op jit(solution)/shard_map/main/pallas_call | solution.py:510
  71.2 3.0 %store.1 = (bf16[2048,1280]{1,0:T(8,128)(2,1)}, f32[1,128]{1,0:T(1,128)}, f32[1,128]{1,0:T(1,128)}, bf16[8,2048]{1,0:T(8,128)(2,1)}) custom-call(bf16[2048,1280]{1,0:T(8,128)(2,1)S(1)} %get-tuple-element.12.gw_ref, f32[1,128]{1,0:T(1,128)S(1)} %get-tuple-element.13.lr_ref, f32[1,128]{1,0:T(1,128)S(1)} %get-tuple-element.14.en_ref, ...), custom_call_target="tpu_custom_call" | custom-call | tf_op jit(solution)/shard_map/store/pallas_call | solution.py:564

commit v6 on v5

--- a/solution.py
+++ b/solution.py
@@ -23,7 +23,9 @@
 CC = 256
 NC = COLS // CC
 TF = 512
-NT = DEPTH // TF
+TILES = ((0, 512, True), (1536, 512, False), (512, 512, True), (1024, 256, True), (1280, 256, True))
+NT = len(TILES)
+RING = (4, 3, 5, 2, 6, 1, 7)
 XF = 1024
 ZF = 512
 DF = DEPTH - XF - ZF
@@ -186,6 +188,20 @@
     row_z = row_of(rank_of(lens, ends_z, slots, True)[0])
     hits = row_z == iota((ROWS, SLOTS), 0)
     pick_ref[...] = onehot(hits)
+
+    def pass_half(w):
+        for g in (0, 1):
+            landed(g, (hx_s.at[w], hx_r.at[w]), x_rows, w * XH, XH).wait_recv()
+            for k in (2, 1, 3):
+                pass_x(g, k, w).start()
+
+    pass_half(0)
+    for g in (0, 1):
+        landed(g, (hz_s, hz_r), z_rows, XF, ZF).wait_recv()
+        for k in RING:
+            pass_z(g, k).start()
+    pass_half(1)
+
     pick_xy = onehot(row_of(rank_of(lens, ends_xy, slots, False)[0]) == iota((ROWS, SLOTS), 0))
     order_ref[...] = lax.dot_general(
         pick_xy, pick_ref[...], (((1,), (1,)), ((), ())), preferred_element_type=F32
@@ -218,19 +234,6 @@
         place = ((by.me - rank) % 8) * 16 + col % 16
         take_ref[i] = onehot(jnp.where(rank >= 0, place, -1) == iota((128, 128), 1))
 
-    def pass_half(w):
-        for g in (0, 1):
-            landed(g, (hx_s.at[w], hx_r.at[w]), x_rows, w * XH, XH).wait_recv()
-            for k in (2, 1, 3):
-                pass_x(g, k, w).start()
-
-    pass_half(0)
-    for g in (0, 1):
-        landed(g, (hz_s, hz_r), z_rows, XF, ZF).wait_recv()
-        for k in (4, 3, 5, 2, 6, 1, 7):
-            pass_z(g, k).start()
-    pass_half(1)
-
     own_copy.wait()
     near_core().wait()
 
@@ -332,13 +335,13 @@
         axis=0,
     )
 
+    stat_peers = [(k, False) for k in RING] + [(k, True) for k in RING + (0,)]
+
     def z_copy(i):
-        k, far = (i + 1, False) if i < 7 else (i - 7, True)
-        return remote(st1, stz.at[i], z_s.at[i], z_r.at[i], z_id(k, far))
+        return remote(st1, stz.at[i], z_s.at[i], z_r.at[i], z_id(*stat_peers[i]))
 
     def xy_copy(i):
-        k, far = (i + 1, False) if i < 7 else (i - 7, True)
-        return remote(st2, stxy.at[i], xy_s.at[i], xy_r.at[i], xy_id(k, far))
+        return remote(st2, stxy.at[i], xy_s.at[i], xy_r.at[i], xy_id(*stat_peers[i]))
 
     for i in range(15):
         z_copy(i).start()
@@ -404,25 +407,16 @@
     by_z.deal, by_z.take, by_z.pack, by_z.give, by_z.get = deal_ref.at[1], take_ref.at[1], pack.at[1], give3.at[1], get3.at[1]
     by_xy.s, by_xy.r, by_z.s, by_z.r = g_s.at[0], g_r.at[0], g_s.at[1], g_r.at[1]
 
+    order = [(t, start, size, by_xy if xy else by_z) for t, (start, size, xy) in enumerate(TILES)]
+
     def first_copy(t, k, by):
-        q = (by.me + k) % 8
+        q, cols = (by.me + k) % 8, pl.ds(0, TILES[t][1])
         return remote(
-            part.at[t, pl.ds(pl.multiple_of(q * 32, 32), 32)], rx1.at[t, k - 1],
+            part.at[t, pl.ds(pl.multiple_of(q * 32, 32), 32), cols], rx1.at[t, k - 1, :, cols],
             a_s.at[t, k - 1], a_r.at[t, k - 1], by.peer(k),
         )
 
-    def partial(t, by):
-        for h in range(TF // 256):
-            part[t, :, h * 256 : h * 256 + 256] = lax.dot_general(
-                by.rows[...], head_v[t * TF + h * 256 : t * TF + h * 256 + 256, :], (((1,), (1,)), ((), ())),
-                preferred_element_type=F32,
-            ).astype(BF16)
-
-        for k in range(1, 8):
-            first_copy(t, k, by).start()
-
-    order = [(0, by_xy), (3, by_z), (1, by_xy), (2, by_xy)]
-    for t, by in order:
+    for t, start, size, by in order:
         if by is by_z:
             def reorder(j, _):
                 cols = pl.ds(pl.multiple_of(j * CC, CC), CC)
@@ -430,7 +424,13 @@
                 return 0
 
             lax.fori_loop(0, NC, reorder, 0)
-        partial(t, by)
+        for h in range(0, size, 256):
+            part[t, :, h : h + 256] = lax.dot_general(
+                by.rows[...], head_v[start + h : start + h + 256, :], (((1,), (1,)), ((), ())),
+                preferred_element_type=F32,
+            ).astype(BF16)
+        for k in RING:
+            first_copy(t, k, by).start()
 
     def head_part(t, _):
         rows = pl.ds(pl.multiple_of(t * 256, 256), 256)
@@ -444,9 +444,9 @@
     en_out[...] = jnp.sum(jnp.where(mask, entropy, 0.0), axis=0, keepdims=True)
 
     def second_copy(t, k, by):
-        q = (by.other + k) % 8
+        q, cols = (by.other + k) % 8, pl.ds(0, TILES[t][1] // 2)
         return remote(
-            s2.at[t, pl.ds(pl.multiple_of(q * 16, 16), 16)], rx2.at[t, k - 1],
+            s2.at[t, pl.ds(pl.multiple_of(q * 16, 16), 16), cols], rx2.at[t, k - 1, :, cols],
             b_s.at[t, k - 1], b_r.at[t, k - 1], by.across(k),
         )
 
@@ -454,32 +454,33 @@
         return remote(by.give.at[(by.me + k) % 8], by.get.at[k], by.s.at[k - 1], by.r.at[k - 1], by.peer(k))
 
     def each(make):
-        for k in range(1, 8):
+        for k in RING:
             make(k)
 
-    for t, by in order:
+    for t, start, size, by in order:
+        half = size // 2
         each(lambda k: first_copy(t, k, by).wait())
-        acc = part[t, pl.ds(pl.multiple_of(by.me * 32, 32), 32)].astype(F32)
+        acc = part[t, pl.ds(pl.multiple_of(by.me * 32, 32), 32), :size].astype(F32)
         for k in range(7):
-            acc = acc + rx1[t, k].astype(F32)
-        both = jnp.concatenate([acc[:, 0:256], acc[:, 256:512]], axis=0).astype(BF16)
-        s2[t] = jnp.dot(by.deal[...], both, preferred_element_type=F32).astype(BF16)
+            acc = acc + rx1[t, k, :, :size].astype(F32)
+        both = jnp.concatenate([acc[:, :half], acc[:, half:]], axis=0).astype(BF16)
+        s2[t, :, :half] = jnp.dot(by.deal[...], both, preferred_element_type=F32).astype(BF16)
         each(lambda k: second_copy(t, k, by).start())
 
     pack[...] = jnp.zeros_like(pack)
-    by_xy.done, by_xy.tiles, by_xy.count = 0, [], 3
-    by_z.done, by_z.tiles, by_z.count = 0, [], 1
-    for t, by in order:
+    for by in (by_xy, by_z):
+        by.chunks, by.last = [], max(o[0] for o in order if o[3] is by)
+    for t, start, size, by in order:
+        half = size // 2
         each(lambda k: second_copy(t, k, by).wait())
-        acc = s2[t, pl.ds(pl.multiple_of(by.other * 16, 16), 16)].astype(F32)
+        acc = s2[t, pl.ds(pl.multiple_of(by.other * 16, 16), 16), :half].astype(F32)
         for k in range(7):
-            acc = acc + rx2[t, k].astype(F32)
+            acc = acc + rx2[t, k, :, :half].astype(F32)
         for h in range(2):
-            for e in range(2):
-                by.pack[:, 4 * by.done + 2 * h + e, :] = acc[8 * h : 8 * h + 8, 128 * e : 128 * e + 128]
-        by.tiles.append(t)
-        by.done += 1
-        if by.done == by.count:
+            for e in range(0, half, 128):
+                by.pack[:, len(by.chunks), :] = acc[8 * h : 8 * h + 8, e : e + 128]
+                by.chunks.append(start + h * half + e)
+        if t == by.last:
             by.give[...] = by.pack[...].astype(BF16)
             each(lambda k: third_copy(k, by).start())
 
@@ -488,18 +489,16 @@
         each(lambda k: third_copy(k, by).wait())
         rows = jnp.dot(by.take[...], by.get[...].reshape(128, 128), preferred_element_type=F32)
         by.pack[...] = rows.reshape(8, 16, 128)
-        for i, t in enumerate(by.tiles):
-            for c in range(4):
-                gh_out[:, t * TF + c * 128 : t * TF + c * 128 + 128] = by.pack[:, 4 * i + c, :]
-
-
-def store_kernel(gw_ref, lr_ref, en_ref, gh_ref, gw_out, lr_out, en_out, gh_out, sem):
-    copy = pltpu.make_async_copy(gw_ref, gw_out, sem.at[0])
-    copy.start()
-    lr_out[...] = lr_ref[...]
-    en_out[...] = en_ref[...]
-    gh_out[...] = gh_ref[...].astype(BF16)
-    copy.wait()
+        for c, start in enumerate(by.chunks):
+            gh_out[:, start : start + 128] = by.pack[:, c, :].astype(BF16)
+
+
+def store_kernel(*refs):
+    copies = [pltpu.make_async_copy(refs[i], refs[4 + i], refs[8].at[i]) for i in range(4)]
+    for c in copies:
+        c.start()
+    for c in copies:
+        c.wait()
 
 
 def local(hidden, head, token_ids, old_logp, advantages, lengths):
@@ -513,7 +512,7 @@
             pltpu.VMEM((DEPTH, COLS), BF16),
             pltpu.VMEM((1, GROUP), F32),
             pltpu.VMEM((1, GROUP), F32),
-            pltpu.VMEM((8, DEPTH), F32),
+            pltpu.VMEM((8, DEPTH), BF16),
         ),
         in_specs=[hbm] * 6,
         out_specs=(vmem,) * 4,
@@ -570,8 +569,8 @@
             jax.ShapeDtypeStruct((8, DEPTH), BF16),
         ),
         in_specs=[vmem] * 4,
-        out_specs=(hbm, vmem, vmem, vmem),
-        scratch_shapes=[dma((1,))],
+        out_specs=(hbm,) * 4,
+        scratch_shapes=[dma((4,))],
         compiler_params=pltpu.CompilerParams(vmem_limit_bytes=32 * 1024 * 1024),
         name="store",
     )(*[keep(a, pltpu.VMEM) for a in (gw, lr, en, gh)])

time: 74.3 us -> 72.7 us (0.978)
  Pallas kernels: 73.6 us -> 71.9 us
    pallas_call x1, Pallas kernels: 70.6 us -> 69.5 us  [local(): pl.pallas_call(main_kernel, out_shape=(pltpu.VMEM((DEPTH, COLS), BF16), p...]
where the time goes in v6:
time: 72.7 us; the launch traced here: 72.6 us
  Pallas kernels  71.9 us (99%)
    pallas_call x1, Pallas kernels, local(): pl.pallas_call(main_kernel, out_shape=(pltpu.VMEM((DEPTH, COLS), BF16), p...  69.5 us
    pallas_call x1, Pallas kernels, local(): pl.pallas_call(store_kernel, out_shape=(jax.ShapeDtypeStruct((DEPTH, COLS...  2.4 us

profile of v6, /device:TPU:8, one launch (start us, length us, event | category | flops | bytes accessed | tf_op | source)
XLA Modules:
  0.0 72.6 jit_solution(14139592833313655922)
XLA Ops:
  0.6 69.5 %main.1 = (bf16[2048,1280]{1,0:T(8,128)(2,1)S(1)}, f32[1,128]{1,0:T(1,128)S(1)}, f32[1,128]{1,0:T(1,128)S(1)}, bf16[8,2048]{1,0:T(8,128)(2,1)S(1)}) custom-call(s32[8]{0:T(128)} %len_hbm.1, s32[1,512]{1,0:T(1,128)} %bitcast.5, f32[1,512]{1,0:T(1,128)} %bitcast.6, f32[1,512]{1,0:T(1,128)} %bitcast.7, bf16[128,8192]{1,0:T(8,128)(2,1)} %hid_ref.1, ...), custom_call_target="tpu_custom_call" | custom-call | tf_op jit(solution)/shard_map/main/pallas_call | solution.py:509
  70.2 2.4 %store.1 = (bf16[2048,1280]{1,0:T(8,128)(2,1)}, f32[1,128]{1,0:T(1,128)}, f32[1,128]{1,0:T(1,128)}, bf16[8,2048]{1,0:T(8,128)(2,1)}) custom-call(bf16[2048,1280]{1,0:T(8,128)(2,1)S(1)} %get-tuple-element.12.refs_0_, f32[1,128]{1,0:T(1,128)S(1)} %get-tuple-element.13.refs_1_, f32[1,128]{1,0:T(1,128)S(1)} %get-tuple-element.14.refs_2_, ...), custom_call_target="tpu_custom_call" | custom-call | tf_op jit(solution)/shard_map/store/pallas_call | solution.py:563

commit v7 on v6

--- a/solution.py
+++ b/solution.py
@@ -27,7 +27,7 @@
 NT = len(TILES)
 RING = (4, 3, 5, 2, 6, 1, 7)
 XF = 1024
-ZF = 512
+ZF = 384
 DF = DEPTH - XF - ZF
 XH = XF // 2
 
@@ -113,13 +113,6 @@
             src_ref=src, dst_ref=dst, send_sem=ss, recv_sem=rs, device_id=dev, device_id_type=MESH
         )
 
-    small = [
-        pltpu.make_async_copy(a, b, loc_sem.at[2 + i])
-        for i, (a, b) in enumerate(((len_hbm, len_ref), (tok_hbm, tok_ref), (old_hbm, old_ref), (adv_hbm, adv_ref)))
-    ]
-    for c in small:
-        c.start()
-
     barrier = pltpu.get_barrier_semaphore()
     for k in range(1, 4):
         pl.semaphore_signal(barrier, inc=1, device_id=dp_id((dp + k) % 4), device_id_type=MESH)
@@ -127,6 +120,13 @@
         for far in (False, True):
             pl.semaphore_signal(barrier, inc=1, device_id=z_id(k, far), device_id_type=MESH)
             pl.semaphore_signal(barrier, inc=1, device_id=xy_id(k, far), device_id_type=MESH)
+    small = [
+        pltpu.make_async_copy(a, b, loc_sem.at[2 + i])
+        for i, (a, b) in enumerate(((len_hbm, len_ref), (tok_hbm, tok_ref), (old_hbm, old_ref), (adv_hbm, adv_ref)))
+    ]
+    for c in small:
+        c.start()
+
     own_copy = pltpu.make_async_copy(
         hid_ref.at[:, pl.ds(pl.multiple_of(dp * DEPTH, DEPTH), DEPTH)], spread.at[dp], loc_sem.at[1]
     )
@@ -299,7 +299,7 @@
         ref = lg.at[j, side, core]
         return remote(ref, ref, sems[0].at[j], sems[1].at[j], dev)
 
-    def full_sum(j, _):
+    def full_sum(j):
         y_copy(j).wait()
         cols = pl.ds(pl.multiple_of(j * CC, CC), CC)
         l = logit[:, cols] + ryy[j]
@@ -307,9 +307,9 @@
         lg[j, y_hi, core] = l
         give(j, (gy_s, gy_r), y_dev, y_hi).start()
         give(j, (gc_s, gc_r), c_dev, y_hi).start()
-        return 0
-
-    lax.fori_loop(0, NC, full_sum, 0)
+
+    for j in range(NC):
+        full_sum(j)
 
     eye = iota((64, 128), 0) + 64 * core == iota((64, 128), 1)
     eye_all = iota((128, 128), 0) == iota((128, 128), 1)
@@ -360,19 +360,19 @@
     for i in range(15):
         xy_copy(i).start()
 
-    def forward(j, _):
+    def forward(j):
         give(j, (gy_s, gy_r), y_dev, 1 - y_hi).wait_recv()
         give(j, (gf_s, gf_r), c_dev, 1 - y_hi).start()
-        return 0
-
-    lax.fori_loop(0, NC, forward, 0)
-    def arrive(j, _):
+
+    for j in range(NC):
+        forward(j)
+    def arrive(j):
         give(j, (gc_s, gc_r), c_dev, y_hi).wait()
         give(j, (gf_s, gf_r), c_dev, 1 - y_hi).wait()
         give(j, (gy_s, gy_r), y_dev, y_hi).wait_send()
-        return 0
-
-    lax.fori_loop(0, NC, arrive, 0)
+
+    for j in range(NC):
+        arrive(j)
     for i in range(15):
         xy_copy(i).wait()
 
@@ -391,16 +391,16 @@
     log_ratio = target - lse - old
     slope = (kl_weight - adv) * jnp.exp(log_ratio) - kl_weight
 
-    def gradient(j, _):
+    def gradient(j):
         l = lg[j].reshape(ROWS, CC)
         hit = iota((ROWS, CC), 1) == tok - (v * COLS + j * CC)
         shifted = l - lse
         probs = jnp.exp(shifted)
         grad = slope * (hit.astype(F32) - probs) + entropy_weight * probs * (shifted + entropy)
         dl_all[:, pl.ds(pl.multiple_of(j * CC, CC), CC)] = grad.astype(BF16)
-        return 0
-
-    lax.fori_loop(0, NC, gradient, 0)
+
+    for j in range(NC):
+        gradient(j)
 
     by_xy.rows, by_z.rows = dl_all, dl_z
     by_xy.deal, by_xy.take, by_xy.pack, by_xy.give, by_xy.get = deal_ref.at[0], take_ref.at[0], pack.at[0], give3.at[0], get3.at[0]

time: 72.7 us -> 71.9 us (0.989)
  Pallas kernels: 71.9 us -> 71.1 us
    pallas_call x1, Pallas kernels: 69.5 us -> 68.7 us  [local(): pl.pallas_call(main_kernel, out_shape=(pltpu.VMEM((DEPTH, COLS), BF16), p...]
where the time goes in v7:
time: 71.9 us; the launch traced here: 71.7 us
  Pallas kernels  71.1 us (99%)
    pallas_call x1, Pallas kernels, local(): pl.pallas_call(main_kernel, out_shape=(pltpu.VMEM((DEPTH, COLS), BF16), p...  68.7 us
    pallas_call x1, Pallas kernels, local(): pl.pallas_call(store_kernel, out_shape=(jax.ShapeDtypeStruct((DEPTH, COLS...  2.4 us

profile of v7, /device:TPU:8, one launch (start us, length us, event | category | flops | bytes accessed | tf_op | source)
XLA Modules:
  0.0 71.7 jit_solution(8341199088897685603)
XLA Ops:
  0.6 68.7 %main.1 = (bf16[2048,1280]{1,0:T(8,128)(2,1)S(1)}, f32[1,128]{1,0:T(1,128)S(1)}, f32[1,128]{1,0:T(1,128)S(1)}, bf16[8,2048]{1,0:T(8,128)(2,1)S(1)}) custom-call(s32[8]{0:T(128)} %len_hbm.1, s32[1,512]{1,0:T(1,128)} %bitcast.5, f32[1,512]{1,0:T(1,128)} %bitcast.6, f32[1,512]{1,0:T(1,128)} %bitcast.7, bf16[128,8192]{1,0:T(8,128)(2,1)} %hid_ref.1, ...), custom_call_target="tpu_custom_call" | custom-call | tf_op jit(solution)/shard_map/main/pallas_call | solution.py:509
  69.3 2.4 %store.1 = (bf16[2048,1280]{1,0:T(8,128)(2,1)}, f32[1,128]{1,0:T(1,128)}, f32[1,128]{1,0:T(1,128)}, bf16[8,2048]{1,0:T(8,128)(2,1)}) custom-call(bf16[2048,1280]{1,0:T(8,128)(2,1)S(1)} %get-tuple-element.12.refs_0_, f32[1,128]{1,0:T(1,128)S(1)} %get-tuple-element.13.refs_1_, f32[1,128]{1,0:T(1,128)S(1)} %get-tuple-element.14.refs_2_, ...), custom_call_target="tpu_custom_call" | custom-call | tf_op jit(solution)/shard_map/store/pallas_call | solution.py:563

commit v8 on v7

--- a/solution.py
+++ b/solution.py
@@ -279,18 +279,14 @@
         cols = pl.ds(pl.multiple_of(j * CC, CC), CC)
         logit[:, cols] = lp[j, y_hi, core] + rxc[j, y_hi]
 
-    def product(j, _):
-        cols = pl.ds(pl.multiple_of(j * CC, CC), CC)
-        lp[j] = jnp.dot(comp[...], head_v[:, cols], preferred_element_type=F32).reshape(2, 2, 64, CC)
+    for j in range(NC):
+        lp[j] = jnp.dot(
+            comp[...], head_v[:, j * CC : j * CC + CC], preferred_element_type=F32
+        ).reshape(2, 2, 64, CC)
         core_copy(j).start()
-
-        @pl.when(j > 0)
-        def _():
+        if j > 0:
             chip_sum(j - 1)
 
-        return 0
-
-    lax.fori_loop(0, NC, product, 0)
     chip_sum(NC - 1)
 
     y_dev, c_dev = dp_id((1 - y_hi) * 2 + core), dp_id(y_hi * 2 + 1 - core)
@@ -335,7 +331,7 @@
         axis=0,
     )
 
-    stat_peers = [(k, False) for k in RING] + [(k, True) for k in RING + (0,)]
+    stat_peers = [(k, True) for k in RING] + [(k, False) for k in RING] + [(0, True)]
 
     def z_copy(i):
         return remote(st1, stz.at[i], z_s.at[i], z_r.at[i], z_id(*stat_peers[i]))
@@ -381,8 +377,8 @@
         lse = top + jnp.log(total)
         return lse, lse - weighted / total, target
 
-    near_rows = row_values([st2[...]] + [stxy[i] for i in range(7)])
-    far_rows = row_values([stxy[i] for i in range(7, 15)])
+    near_rows = row_values([st2[...]] + [stxy[i] for i in range(7, 14)])
+    far_rows = row_values([stxy[i] for i in (0, 1, 2, 3, 4, 5, 6, 14)])
     low = y_hi == 0
     lse, entropy, target = [
         jnp.concatenate([to_col(jnp.where(low, a, b)), to_col(jnp.where(low, b, a))], axis=0)

time: 71.9 us -> 72.7 us (1.011)
  no operation moved by 1% of the time
where the time goes in v8:
time: 72.7 us; the launch traced here: 72.3 us
  Pallas kernels  71.6 us (98%)
    pallas_call x1, Pallas kernels, local(): pl.pallas_call(main_kernel, out_shape=(pltpu.VMEM((DEPTH, COLS), BF16), p...  69.2 us
    pallas_call x1, Pallas kernels, local(): pl.pallas_call(store_kernel, out_shape=(jax.ShapeDtypeStruct((DEPTH, COLS...  2.4 us

profile of v8, /device:TPU:8, one launch (start us, length us, event | category | flops | bytes accessed | tf_op | source)
XLA Modules:
  0.0 72.3 jit_solution(9516820092735272449)
XLA Ops:
  0.6 69.2 %main.1 = (bf16[2048,1280]{1,0:T(8,128)(2,1)S(1)}, f32[1,128]{1,0:T(1,128)S(1)}, f32[1,128]{1,0:T(1,128)S(1)}, bf16[8,2048]{1,0:T(8,128)(2,1)S(1)}) custom-call(s32[8]{0:T(128)} %len_hbm.1, s32[1,512]{1,0:T(1,128)} %bitcast.5, f32[1,512]{1,0:T(1,128)} %bitcast.6, f32[1,512]{1,0:T(1,128)} %bitcast.7, bf16[128,8192]{1,0:T(8,128)(2,1)} %hid_ref.1, ...), custom_call_target="tpu_custom_call" | custom-call | tf_op jit(solution)/shard_map/main/pallas_call | solution.py:505
  69.9 2.4 %store.1 = (bf16[2048,1280]{1,0:T(8,128)(2,1)}, f32[1,128]{1,0:T(1,128)}, f32[1,128]{1,0:T(1,128)}, bf16[8,2048]{1,0:T(8,128)(2,1)}) custom-call(bf16[2048,1280]{1,0:T(8,128)(2,1)S(1)} %get-tuple-element.12.refs_0_, f32[1,128]{1,0:T(1,128)S(1)} %get-tuple-element.13.refs_1_, f32[1,128]{1,0:T(1,128)S(1)} %get-tuple-element.14.refs_2_, ...), custom_call_target="tpu_custom_call" | custom-call | tf_op jit(solution)/shard_map/store/pallas_call | solution.py:559
